TPU v7x, 128 devices: a whole 4x4x4 slice. The times are simulated.
128 devices in a mesh: prow: 4 (over y), pcol: 32 (over x, z, core).
Axes of the slice: x: 4, y: 4, z: 4, core: 2. Of those that a mesh axis runs over, the one named last changes fastest.
Arguments:
- matrix: float32 [16, 4, 128, 12, 32, 128], P(None, 'prow', None, None, 'pcol'), may hold values from -240 to 240, as said below
- pivots: int32 [2, 128], replicated, may hold values from 0 to 8191, as said below
Outputs:
- factored: float32 [16, 4, 128, 12, 32, 128], P(None, 'prow', None, None, 'pcol')
Inputs may be any that keep to these rules, and one draw needn't show every extreme that they name: pivots[s] lists 128 distinct rows, each s * 128 or more; 8191 is among them, and row 0 is among those of pivots[0]. `matrix`: swapping by the listed rows leaves diagonal blocks whose factorization without further pivoting is well conditioned.
All inputs are finite; a program needn't handle non-finite values.
Results may differ from a plain program's by a relative error of at most 0.0001.
Values sent between devices are 32-bit elements; how exact they have to be, the bound alone decides.
A program may use at most 192 MiB of HBM per device.

v0:
```python
import jax
import jax.numpy as jnp
from jax import lax
from jax.experimental import pallas as pl
from jax.experimental.pallas import tpu as pltpu
from jax.sharding import PartitionSpec as P

NB = 128
F32 = jnp.float32
BF16 = jnp.bfloat16
MESH = pl.DeviceIdType.MESH
SLOTS_A = 96
SLOTS_D = 64
LOADS = 8
(
    OWNER, LOCAL, OVER, ARR_LOCAL, ARR_COUNT, OUT_LOCAL, OUT_SLOT, OUT_COUNT,
    IN_TARGET, IN_ROW, IN_LINE, IN_ORIGIN, IN_COUNT,
) = range(13)


def split(x):
    high = x.astype(BF16)
    return high, (x - high.astype(F32)).astype(BF16)


def dot(a, b):
    return jnp.dot(a, b, preferred_element_type=F32)


def dot3(a, b):
    ah, al = a
    bh, bl = b
    return dot(ah, bh) + (dot(ah, bl) + dot(al, bh))


def onehot_rows(onehot, x):
    high = x.astype(BF16)
    rest = x - high.astype(F32)
    mid = rest.astype(BF16)
    low = (rest - mid.astype(F32)).astype(BF16)
    return (dot(onehot, high) + dot(onehot, mid)) + dot(onehot, low)


def iota(shape, dim):
    return lax.broadcasted_iota(jnp.int32, shape, dim)


def eliminate(a_ref, xl_ref, xu_ref, t_ref, index, half):
    local = pl.multiple_of(index * 16, 16)
    start = pl.multiple_of(half * NB + local, 16)
    sub = iota((16, NB), 0)
    lane = iota((16, NB), 1)
    original = [a_ref[g, pl.ds(start, 16), :] for g in range(2)]
    rolled = pltpu.roll(original[half], lax.rem(NB - local, NB), axis=1)
    cols = [jnp.broadcast_to(rolled[:, j : j + 1], (16, NB)) for j in range(16)]
    upper = list(original[half:])
    jordan = list(original[half:])
    ident = jnp.where((lane == sub) | (lane == sub + 16), 1.0, 0.0).astype(F32)
    factors = jnp.zeros((16, NB), F32)
    scale = jnp.zeros((16, NB), F32)

    def pick(x, k):
        return jnp.broadcast_to(x[k : k + 1, :], (16, NB))

    for k in range(16):
        inverse = 1.0 / pick(cols[k], k)
        mult = cols[k] * inverse
        low = jnp.where(sub > k, mult, 0.0)
        both = jnp.where(sub != k, mult, 0.0)
        for j in range(k + 1, 16):
            cols[j] = cols[j] - both * pick(cols[j], k)
        upper = [x - low * pick(x, k) for x in upper]
        jordan = [x - both * pick(x, k) for x in jordan]
        mixed = jnp.where(lane < 16, low, both - low)
        ident = ident - mixed * pick(ident, k)
        factors = jnp.where((lane == local + k) & (sub > k), mult, factors)
        scale = jnp.where(sub == k, inverse, scale)

    in_block = (lane >= local) & (lane < local + 16)
    lower_of_block = in_block & (lane - local < sub)
    merged = jnp.where(lower_of_block, factors, jnp.where(lane < local, original[half], upper[0]))
    a_ref[half, pl.ds(start, 16), :] = merged
    if half == 0:
        a_ref[1, pl.ds(start, 16), :] = upper[1]
    left_inv = pltpu.roll(jnp.where(lane < 16, ident, 0.0), local, axis=1)
    right_inv = pltpu.roll(
        jnp.where((lane >= 16) & (lane < 32), ident * scale, 0.0), lax.rem(local + NB - 16, NB), axis=1
    )
    zero = jnp.zeros((16, NB), F32)
    xl_ref[half, pl.ds(start, 16), :] = left_inv
    xl_ref[1 - half, pl.ds(start, 16), :] = zero
    xu_ref[half, pl.ds(start, 16), :] = right_inv
    xu_ref[1 - half, pl.ds(start, 16), :] = zero

    t_ref[0, pl.ds(local, 16), :] = jnp.where(
        lane >= local + 16, jordan[0] * scale, jnp.where(in_block, right_inv, 0.0)
    )
    if half == 0:
        t_ref[1, pl.ds(local, 16), :] = jordan[1] * scale
    rows = 2 * NB - half * NB
    below = iota((rows, NB), 0) + half * NB >= start + 16
    wide_lane = iota((rows, NB), 1)
    block_lane = (wide_lane >= local) & (wide_lane < local + 16)
    panel = a_ref[half, half * NB :, :]
    panel_parts = split(panel)
    product = dot3(panel_parts, split(t_ref[0]))
    a_ref[half, half * NB :, :] = jnp.where(
        below, jnp.where(block_lane, product, panel - product), panel
    )
    if half == 0:
        other = a_ref[1]
        product = dot3(panel_parts, split(t_ref[1]))
        a_ref[1] = jnp.where(below, other - product, other)
    t_ref[0, pl.ds(local, 16), :] = zero
    if half == 0:
        t_ref[1, pl.ds(local, 16), :] = zero


def lu_core(a_ref, xl_ref, xu_ref, t_ref):
    t_ref[...] = jnp.zeros(t_ref.shape, F32)
    for half in range(2):
        def step(index, carry, half=half):
            eliminate(a_ref, xl_ref, xu_ref, t_ref, index, half)
            return carry
        lax.fori_loop(0, 8, step, 0)
    packed = jnp.concatenate([a_ref[0], a_ref[1]], 1)
    left = jnp.concatenate([xl_ref[0], xl_ref[1]], 1)
    right = jnp.concatenate([xu_ref[0], xu_ref[1]], 1)
    row = iota((256, 256), 0)
    col = iota((256, 256), 1)
    size = 16
    while size < 256:
        pair = row // (2 * size) == col // (2 * size)
        low_corner = pair & (row % (2 * size) >= size) & (col % (2 * size) < size)
        up_corner = pair & (row % (2 * size) < size) & (col % (2 * size) >= size)
        left_parts = split(left)
        right_parts = split(right)
        first = dot3(left_parts, split(jnp.where(low_corner, packed, 0.0)))
        second = dot3(right_parts, split(jnp.where(up_corner, packed, 0.0)))
        left = left - dot3(split(first), left_parts)
        right = right - dot3(split(second), right_parts)
        size *= 2
    return packed, left, right


def lu_kernel(arr_ref, slot_ref, packed_ref, linv_ref, uinv_ref, a_ref, xl_ref, xu_ref, t_ref):
    count = arr_ref.shape[1]
    slot = slot_ref[:, :1]
    onehot = jnp.where(iota((256, count), 1) == slot, 1.0, 0.0).astype(BF16)
    for half in range(2):
        a_ref[half] = onehot_rows(onehot, arr_ref[half])
    packed, left, right = lu_core(a_ref, xl_ref, xu_ref, t_ref)
    packed_ref[...] = packed
    linv_ref[...] = left
    uinv_ref[...] = right


def lu_call(arr, slot_col):
    square = jax.ShapeDtypeStruct((256, 256), F32)
    whole = pl.BlockSpec((256, 256), lambda i: (0, 0))
    return pl.pallas_call(
        lu_kernel,
        grid=(1,),
        in_specs=[
            pl.BlockSpec((2, 4 * SLOTS_A, NB), lambda i: (0, 0, 0)),
            pl.BlockSpec((256, NB), lambda i: (0, 0)),
        ],
        out_specs=[whole] * 3,
        out_shape=[square] * 3,
        scratch_shapes=[pltpu.VMEM((2, 256, 128), F32)] * 3 + [pltpu.VMEM((2, 128, 128), F32)],
        compiler_params=pltpu.CompilerParams(vmem_limit_bytes=32 * 2**20),
        name="factor",
    )(arr, slot_col)


def index_kernel(piv_ref, idx_ref, slot_ref):
    lane = iota((NB, NB), 1).astype(F32)
    sub = iota((NB, NB), 0).astype(F32)

    def rows(x):
        return jnp.broadcast_to(x, (NB, NB))

    def lanes_sum(cond, value=1.0):
        return rows(jnp.sum(jnp.where(cond, value, 0.0), axis=1, keepdims=True))

    def subs_sum(cond, value=1.0):
        return rows(jnp.sum(jnp.where(cond, value, 0.0), axis=0, keepdims=True))

    given = piv_ref[...].astype(F32)
    row = [rows(given[s : s + 1, :]) for s in range(2)]
    col = [x.T for x in row]
    fill_row, fill_col = [], []
    for s in range(2):
        start = float(s * NB)
        listed_row = subs_sum(col[s] == lane + start)
        listed_col = lanes_sum(row[s] == sub + start)
        rank_vacated = lanes_sum((lane <= sub) & (row[s] >= start + NB))
        rank_displaced = subs_sum((sub <= lane) & (listed_col == 0.0))
        pairing = (col[s] >= start + NB) & (listed_row == 0.0) & (rank_vacated == rank_displaced)
        filler = lanes_sum(pairing, lane + start)
        fill_col.append(filler)
        fill_row.append(filler.T)
    again = col[1] == row[0]
    source_col = jnp.where(lanes_sum(again) > 0.0, lanes_sum(again, fill_row[0]), col[1])
    moved = fill_col[1] == row[0]
    second_col = jnp.where(lanes_sum(moved) > 0.0, lanes_sum(moved, fill_row[0]), fill_col[1])

    def whole(x):
        return x.astype(jnp.int32)

    def place(value):
        number = whole(value)
        return (number >> 7) & 3, (number >> 9) * NB + (number & (NB - 1))

    def ranks(keys):
        keys_row = [k.astype(F32) for k in keys]
        keys_col = [k.T for k in keys_row]
        first = subs_sum((keys_col[0] == keys_row[0]) & (sub < lane))
        second = subs_sum((keys_col[1] == keys_row[1]) & (sub < lane)) + subs_sum(
            keys_col[0] == keys_row[1]
        )
        return [whole(first), whole(second)]

    sources = [row[0], source_col.T]
    owners, locals_ = zip(*[place(x) for x in sources])
    rank_arr = ranks(owners)
    slots = [o * SLOTS_A + r for o, r in zip(owners, rank_arr)]
    valid = [(row[0] >= 2.0 * NB) & (subs_sum(again) == 0.0), row[1] >= 2.0 * NB]
    origins = [whole(fill_row[0]), whole(second_col.T)]
    dests, targets = zip(*[place(x) for x in row])
    halves = [x >> 7 for x in origins]
    keys = [jnp.where(v, h * 4 + d, 9) for v, h, d in zip(valid, halves, dests)]
    rank_disp = ranks(keys)
    zero = jnp.zeros((NB, NB), jnp.int32)
    over = zero
    for g in range(2):
        over = over + whole(rows(jnp.sum(jnp.where(rank_arr[g] >= SLOTS_A, 1.0, 0.0), axis=1, keepdims=True)))
        bad = valid[g] & (rank_disp[g] >= SLOTS_D)
        over = over + whole(rows(jnp.sum(jnp.where(bad, 1.0, 0.0), axis=1, keepdims=True)))
    me = lax.axis_index("prow")

    def compact(chosen, values):
        chosen = [jnp.where(c, 1.0, 0.0) for c in chosen]
        chosen_col = [c.T for c in chosen]
        first = subs_sum((chosen_col[0] > 0.0) & (sub < lane))
        total = subs_sum(chosen_col[0] > 0.0)
        second = subs_sum((chosen_col[1] > 0.0) & (sub < lane)) + total
        order = [jnp.where(c > 0.0, r, -1.0).T for c, r in zip(chosen, (first, second))]
        packed = []
        for value in values:
            value_col = [v.astype(F32).T for v in value]
            packed.append(
                [
                    whole(sum(subs_sum(o == lane + g * NB, v) for o, v in zip(order, value_col)))
                    for g in range(2)
                ]
            )
        count = whole(total + subs_sum(chosen_col[1] > 0.0))
        return packed, [count, count]

    (arr_local,), arr_count = compact([o == me for o in owners], [locals_])
    (out_local, out_slot), out_count = compact(
        [v & (h == me) for v, h in zip(valid, halves)],
        [
            [x & (NB - 1) for x in origins],
            [d * SLOTS_D + r for d, r in zip(dests, rank_disp)],
        ],
    )
    (in_target, in_row, in_line, in_origin), in_count = compact(
        [v & (d == me) for v, d in zip(valid, dests)],
        [
            targets,
            [h * NB + r for h, r in zip(halves, rank_disp)],
            [h * SLOTS_D + r for h, r in zip(halves, rank_disp)],
            origins,
        ],
    )
    fields = [
        owners, locals_, [over, over], arr_local, arr_count, out_local, out_slot, out_count,
        in_target, in_row, in_line, in_origin, in_count,
    ]
    for number, field in enumerate(fields):
        for g in range(2):
            idx_ref[number : number + 1, g * NB : (g + 1) * NB] = field[g][0:1, :]
    for number in range(len(fields), 16):
        idx_ref[number : number + 1, :] = jnp.zeros((1, 2 * NB), jnp.int32)
    for g in range(2):
        slot_ref[g * NB : (g + 1) * NB, :] = whole(slots[g].astype(F32).T)


def index_call(pivots):
    return pl.pallas_call(
        index_kernel,
        out_shape=[
            jax.ShapeDtypeStruct((16, 2 * NB), jnp.int32),
            jax.ShapeDtypeStruct((2 * NB, NB), jnp.int32),
        ],
        name="indices",
    )(pivots)


def gather_kernel(idx_ref, x_ref, arr_ref, disp_ref, arr_line_ref, disp_line_ref, raw_ref, whole, sems):
    me = lax.axis_index("prow")
    lines = whole.shape[0] // (16 * NB)
    part = whole.shape[0] // LOADS
    loads = []
    for number in range(LOADS):
        here = pl.ds(number * part, part)
        loads.append(pltpu.make_async_copy(x_ref.at[here], whole.at[here], sems.at[number]))
        loads[-1].start()
    arr_ref[...] = jnp.zeros(arr_ref.shape, F32)
    for load in loads:
        load.wait()

    def arriving(j, carry):
        arr_ref[pl.ds(j * lines, lines), :] = whole[pl.ds(idx_ref[ARR_LOCAL, j] * lines, lines), :]
        return carry

    def displaced(t, carry):
        disp_ref[pl.ds(idx_ref[OUT_SLOT, t] * lines, lines), :] = whole[
            pl.ds(idx_ref[OUT_LOCAL, t] * lines, lines), :
        ]
        return carry

    lax.fori_loop(0, idx_ref[ARR_COUNT, 0], arriving, 0)
    lax.fori_loop(0, idx_ref[OUT_COUNT, 0], displaced, 0)
    arr_line_ref[...] = arr_ref[pl.ds(0, SLOTS_A, lines), :]
    disp_line_ref[...] = disp_ref[pl.ds(0, 4 * SLOTS_D, lines), :]
    raw_ref[...] = whole[pl.ds(0, 16 * NB, lines), :]


ANY = pl.BlockSpec(memory_space=pl.ANY)


def gather_call(idx, x, lines):
    sizes = [SLOTS_A * lines, 4 * SLOTS_D * lines, SLOTS_A, 4 * SLOTS_D, 16 * NB]
    vmem = pl.BlockSpec(memory_space=pltpu.VMEM)
    return pl.pallas_call(
        gather_kernel,
        in_specs=[pl.BlockSpec(memory_space=pltpu.SMEM), ANY],
        out_specs=[vmem] * 5,
        out_shape=[jax.ShapeDtypeStruct((size, NB), F32) for size in sizes],
        scratch_shapes=[pltpu.VMEM(x.shape, F32), pltpu.SemaphoreType.DMA((LOADS,))],
        compiler_params=pltpu.CompilerParams(vmem_limit_bytes=40 * 2**20),
        name="gather",
    )(idx, x)


DISP_LINES = 4 * SLOTS_A
RAW_LINES = DISP_LINES + 2 * NB
TREE_BLOCKS = 5


def rows8(start, size):
    return pl.ds(pl.multiple_of(start, 8), size)


def exchange_kernel(
    arr_ref, disp_ref, arr_line_ref, disp_line_ref, raw_ref, recv_arr, recv_disp, panel, relay,
    local_sem, y_send, y_recv, p_send, p_recv, t_send, t_recv, s_send, s_recv,
):
    p = lax.axis_index("prow")
    q = lax.axis_index("pcol")
    cx, cz, core = q // 8, (q // 2) % 4, q % 2
    root = q < 2

    def column(ix, iz, icore):
        return ((ix + 4) % 4 * 4 + (iz + 4) % 4) * 2 + icore

    up, down, across = ((p + 1) % 4, q), ((p + 3) % 4, q), ((p + 2) % 4, q)
    sibling = (p, column(cx, cz, 1 - core))
    near = [
        up, down, across, sibling,
        (p, column(cx + 1, cz, core)), (p, column(cx + 3, cz, core)),
        (p, column(cx, cz + 1, core)), (p, column(cx, cz + 3, core)),
    ]
    barrier = pltpu.get_barrier_semaphore()
    for other in near:
        pl.semaphore_signal(barrier, inc=1, device_id=other, device_id_type=MESH)
    pl.semaphore_wait(barrier, len(near))

    def remote(src, dst, send, recv, device):
        return pltpu.make_async_remote_copy(
            src_ref=src, dst_ref=dst, send_sem=send, recv_sem=recv, device_id=device, device_id_type=MESH
        )

    def arr_lines(owner):
        return panel.at[core, rows8(owner * SLOTS_A, SLOTS_A)]

    def disp_lines(half):
        return panel.at[core, rows8(DISP_LINES + half * SLOTS_D, SLOTS_D)]

    def disp_for(owner):
        return disp_line_ref.at[rows8(owner * SLOTS_D, SLOTS_D)]

    peers = [up, down, across]
    own_raw = pltpu.make_async_copy(raw_ref, panel.at[core, pl.ds(RAW_LINES, 16 * NB)], local_sem.at[0])
    own_arr = pltpu.make_async_copy(arr_line_ref, arr_lines(p), local_sem.at[1])
    own_disp = pltpu.make_async_copy(disp_for(p), disp_lines(p % 2), local_sem.at[2])
    arr_panel = [
        remote(arr_line_ref, arr_lines(p), p_send.at[i], p_recv.at[i], peers[i]) for i in range(3)
    ]
    disp_panel = [
        remote(disp_for(peers[i][0]), disp_lines(p % 2), p_send.at[3 + i], p_recv.at[3 + p % 2], peers[i])
        for i in range(3)
    ]

    @pl.when(root)
    def _():
        for copy in arr_panel:
            copy.start()

        @pl.when(p < 2)
        def _():
            for copy in disp_panel:
                copy.start()
            own_disp.start()

        own_arr.start()
        own_raw.start()

    arr_size, disp_size = arr_ref.shape[0], disp_ref.shape[0] // 4
    half_size = arr_size // 2
    low, high = pl.ds(0, half_size), pl.ds(half_size, half_size)

    def arr_rows(owner, part):
        return recv_arr.at[rows8(owner * arr_size + part.start, part.size)]

    def moved_to(owner):
        return disp_ref.at[rows8(owner * disp_size, disp_size)]

    def moved(half):
        return recv_disp.at[rows8(half * (recv_disp.shape[0] // 2), disp_size)]

    own_rows = pltpu.make_async_copy(arr_ref, recv_arr.at[rows8(p * arr_size, arr_size)], local_sem.at[3])
    own_moved = pltpu.make_async_copy(moved_to(p), moved(p % 2), local_sem.at[4])
    bulk = [
        remote(arr_ref.at[low], arr_rows(p, low), y_send.at[0], y_recv.at[0], up),
        remote(arr_ref.at[high], arr_rows(p, high), y_send.at[1], y_recv.at[1], down),
        remote(arr_ref.at[high], arr_rows(p, high), y_send.at[2], y_recv.at[2], up),
        remote(arr_ref.at[low], arr_rows(p, low), y_send.at[3], y_recv.at[3], down),
    ]
    for copy in bulk:
        copy.start()
    own_rows.start()

    half = p % 2
    to_up = remote(moved_to(up[0]), moved(half), y_send.at[4], y_recv.at[4 + half], up)
    to_down = remote(moved_to(down[0]), moved(half), y_send.at[5], y_recv.at[4 + half], down)
    via = [
        remote(moved_to(2), relay, y_send.at[6], y_recv.at[6], down),
        remote(moved_to(3), relay, y_send.at[6], y_recv.at[6], up),
    ]

    @pl.when(p < 2)
    def _():
        to_up.start()
        to_down.start()
        own_moved.start()

    for number in range(2):
        @pl.when(p == number)
        def _(number=number):
            via[number].start()

    forward = [
        remote(arr_rows(down[0], low), arr_rows(down[0], low), y_send.at[7], y_recv.at[7], up),
        remote(arr_rows(up[0], high), arr_rows(up[0], high), y_send.at[8], y_recv.at[8], down),
    ]

    def block(which, stream, k):
        line = jnp.where(k == 0, stream * NB, RAW_LINES + (stream * (TREE_BLOCKS - 1) + k - 1) * NB)
        return panel.at[which, pl.ds(pl.multiple_of(line, NB), NB)]

    def along(stream):
        sign = 1 if stream % 2 == 0 else 3
        return sign, (cx * sign) % 4, (cz * sign) % 4

    def tree(stream, k):
        sign, ax, az = along(stream)
        next_x = (p, column(cx + sign, cz, core))
        next_z = (p, column(cx, cz + sign, core))
        first, second = (ax, az) if stream < 2 else (az, ax)
        to_first, to_second = (next_x, next_z) if stream < 2 else (next_z, next_x)
        number = stream * TREE_BLOCKS + k
        ref = block(core, stream, k)
        return (
            (second == 0) & (first < 3),
            remote(ref, ref, t_send.at[0, number], t_recv.at[number], to_first),
            second < 3,
            remote(ref, ref, t_send.at[1, number], t_recv.at[number], to_second),
            remote(ref, ref, s_send.at[number], s_recv.at[number], sibling),
        )

    def pass_on(stream, step):
        _, ax, az = along(stream)
        depth = ax + az
        k = step - depth

        @pl.when((k >= 0) & (k < TREE_BLOCKS))
        def _():
            go_first, send_first, go_second, send_second, send_sibling = tree(stream, k)

            @pl.when(depth > 0)
            def _():
                send_first.wait_recv()

            @pl.when(go_first)
            def _():
                send_first.start()

            @pl.when(go_second)
            def _():
                send_second.start()

            send_sibling.start()

    @pl.when(root)
    def _():
        own_arr.wait()
        for copy in arr_panel:
            copy.wait_recv()
        for source in range(2):
            @pl.when(p == source)
            def _():
                own_disp.wait()

            @pl.when(p != source)
            def _(source=source):
                remote(disp_for(0), disp_lines(source), p_send.at[3], p_recv.at[3 + source], up).wait_recv()
        own_raw.wait()

    def tree_step(step, carry):
        for stream in range(4):
            pass_on(stream, step)
        return carry

    lax.fori_loop(0, 6, tree_step, 0)
    bulk[0].wait_recv()
    forward[0].start()
    bulk[1].wait_recv()
    forward[1].start()
    lax.fori_loop(6, 6 + TREE_BLOCKS, tree_step, 0)
    for number in range(2):
        @pl.when(p == 3 - number)
        def _(number=number):
            target = (2, q) if number == 0 else (3, q)
            remote(relay, relay, y_send.at[6], y_recv.at[6], target).wait_recv()
            onward = remote(relay, moved(number), y_send.at[9], y_recv.at[4 + number], target)
            onward.start()
            onward.wait_send()
    bulk[2].wait_recv()
    bulk[3].wait_recv()
    for copy in forward:
        copy.wait_recv()
    own_rows.wait()
    for source in range(2):
        @pl.when(p == source)
        def _():
            own_moved.wait()

        @pl.when(p != source)
        def _(source=source):
            remote(moved_to(0), moved(source), y_send.at[4], y_recv.at[4 + source], up).wait_recv()
    for copy in bulk + forward:
        copy.wait_send()

    @pl.when(p < 2)
    def _():
        to_up.wait_send()
        to_down.wait_send()
        via[0].wait_send()

    def finish(k, carry):
        for stream in range(4):
            go_first, send_first, go_second, send_second, send_sibling = tree(stream, k)

            @pl.when(go_first)
            def _():
                send_first.wait_send()

            @pl.when(go_second)
            def _():
                send_second.wait_send()

            send_sibling.wait_send()
            send_sibling.wait_recv()
        return carry

    lax.fori_loop(0, TREE_BLOCKS, finish, 0)

    @pl.when(root)
    def _():
        for copy in arr_panel:
            copy.wait_send()

        @pl.when(p < 2)
        def _():
            for copy in disp_panel:
                copy.wait_send()


def exchange_call(operands, lines):
    dma = pltpu.SemaphoreType.DMA
    sizes = [(4 * SLOTS_A * lines,), (2 * NB * lines,), (2, RAW_LINES + 16 * NB), (SLOTS_D * lines,)]
    return pl.pallas_call(
        exchange_kernel,
        in_specs=[pl.BlockSpec(memory_space=pltpu.VMEM)] * 5,
        out_specs=[ANY] * 4,
        out_shape=[jax.ShapeDtypeStruct(size + (NB,), F32) for size in sizes],
        scratch_shapes=[
            dma((5,)), dma((10,)), dma((9,)), dma((6,)), dma((5,)), dma((2, 20)), dma((20,)), dma((20,)), dma((20,)),
        ],
        compiler_params=pltpu.CompilerParams(collective_id=0, has_side_effects=True),
        name="exchange",
    )(*operands)


STEP_ROWS = 256


def update_kernel(
    idx_ref, x_ref, panel_ref, disp_ref, arr_ref, slot_ref, packed_ref, linv_ref, uinv_ref, o_ref,
    whole, pan, stacked, u_ref, x_sem, pan_sem,
):
    p = lax.axis_index("prow")
    q = lax.axis_index("pcol")
    step = pl.program_id(0)
    lines = whole.shape[0] // (16 * NB)

    @pl.when(step == 0)
    def _():
        load = pltpu.make_async_copy(x_ref, whole, x_sem)
        load.start()
        load_panel = pltpu.make_async_copy(panel_ref, pan, pan_sem)
        load_panel.start()
        high, low = split(linv_ref[...])
        slot = slot_ref[:, :1]
        onehot = jnp.where(iota((2 * NB, 4 * SLOTS_A), 1) == slot, 1.0, 0.0).astype(BF16)
        left = (dot(high, onehot).astype(BF16), dot(low, onehot).astype(BF16))
        for c in range(lines):
            rows = arr_ref[pl.ds(c, 4 * SLOTS_A, lines), :]
            value = dot3(left, split(rows))
            here = slice(c * NB, (c + 1) * NB)
            u_ref[:, here] = value
            upper, rest = split(value)
            stacked[0 : 2 * NB, here] = upper
            stacked[2 * NB : 4 * NB, here] = rest
            stacked[4 * NB : 6 * NB, here] = upper
        load_panel.wait()
        load.wait()

        def patch(t, carry):
            target = idx_ref[IN_TARGET, t]
            line = idx_ref[IN_LINE, t] + DISP_LINES
            for half in range(2):
                pan[half, pl.ds(RAW_LINES + target, 1), :] = pan[half, pl.ds(line, 1), :]
            source = idx_ref[IN_ROW, t] * lines
            whole[pl.ds(target * lines, lines), :] = disp_ref[pl.ds(source, lines), :]
            return carry

        lax.fori_loop(0, idx_ref[IN_COUNT, 0], patch, 0)

    here = pl.ds(pl.multiple_of(RAW_LINES + step * STEP_ROWS, NB), STEP_ROWS)
    rows = jnp.concatenate([pan[0, here, :], pan[1, here, :]], 1)
    mult = dot3(split(rows), split(uinv_ref[...]))
    high, low = split(mult)
    left = jnp.concatenate([high, high, low], 1)
    base = step * (STEP_ROWS * lines)
    for c in range(0, lines, 2):
        product = dot(left, stacked[:, c * NB : (c + 2) * NB])
        for k in range(2):
            current = whole[pl.ds(base + c + k, STEP_ROWS, lines), :]
            o_ref[pl.ds(c + k, STEP_ROWS, lines), :] = current - product[:, k * NB : (k + 1) * NB]

    for half in range(2):
        @pl.when(q == half)
        def _(half=half):
            o_ref[pl.ds(0, STEP_ROWS, lines), :] = mult[:, half * NB : (half + 1) * NB]

    for half in range(2):
        @pl.when((p == half) & (step == 0))
        def _(half=half):
            top = slice(half * NB, (half + 1) * NB)
            for c in range(lines):
                value = u_ref[top, c * NB : (c + 1) * NB]
                if c == 0:
                    value = jnp.where(q == 0, packed_ref[top, :NB], jnp.where(q == 1, packed_ref[top, NB:], value))
                o_ref[pl.ds(c, NB, lines), :] = value


def update_call(idx, x, panel, disp, arr, slot, packed, linv, uinv, lines):
    vmem = pl.BlockSpec(memory_space=pltpu.VMEM)
    return pl.pallas_call(
        update_kernel,
        grid=(16 * NB // STEP_ROWS,),
        in_specs=[pl.BlockSpec(memory_space=pltpu.SMEM), ANY, ANY] + [vmem] * 6,
        out_specs=pl.BlockSpec((STEP_ROWS * lines, NB), lambda i: (i, 0)),
        out_shape=jax.ShapeDtypeStruct((16 * NB * lines, NB), F32),
        scratch_shapes=[
            pltpu.VMEM((16 * NB * lines, NB), F32),
            pltpu.VMEM((2, RAW_LINES + 16 * NB, NB), F32),
            pltpu.VMEM((6 * NB, NB * lines), BF16),
            pltpu.VMEM((2 * NB, NB * lines), F32),
            pltpu.SemaphoreType.DMA,
            pltpu.SemaphoreType.DMA,
        ],
        compiler_params=pltpu.CompilerParams(vmem_limit_bytes=48 * 2**20),
        name="update",
    )(idx, x, panel, disp, arr, slot, packed, linv, uinv)


def shards(matrix, pivots):
    lines = matrix.shape[3]
    rows = matrix.shape[0] * NB
    p = lax.axis_index("prow")
    q = lax.axis_index("pcol")
    x = matrix.reshape(rows * lines, NB)
    idx, slot = index_call(pivots)

    def fits(x, idx, slot):
        recv_arr, recv_disp, panel, _ = exchange_call(gather_call(idx, x, lines), lines)
        return recv_arr, recv_disp, panel, idx, slot

    def general(x, idx, slot):
        x = x.reshape(rows, lines, NB)
        chosen = jnp.where((idx[OWNER] == p)[:, None, None], jnp.take(x, idx[LOCAL], axis=0), 0.0)
        top = jnp.concatenate([jnp.where(p == s, x[:NB], 0.0) for s in range(2)])
        chosen, top = lax.psum((chosen, top), "prow")
        chosen = jnp.pad(chosen, ((0, 4 * SLOTS_A - 2 * NB), (0, 0), (0, 0)))
        own = jnp.concatenate([chosen[:, 0], top[:, 0], x[:, 0]])
        panel = lax.psum(jnp.stack([jnp.where(q == s, own, 0.0) for s in range(2)]), "pcol")
        order = jnp.arange(2 * NB, dtype=jnp.int32)
        idx = idx.at[IN_ROW].set(idx[IN_ORIGIN]).at[IN_LINE].set(idx[IN_ORIGIN])
        slot = jnp.broadcast_to(order[:, None], slot.shape)
        return chosen.reshape(-1, NB), top.reshape(-1, NB), panel, idx, slot

    arr, disp, panel, idx, slot = lax.cond(idx[OVER, 0] == 0, fits, general, x, idx, slot)
    packed, linv, uinv = lu_call(panel, slot)
    out = update_call(idx, x, panel, disp, arr, slot, packed, linv, uinv, lines)
    return out.reshape(matrix.shape)


def solution(mesh):
    placed = (P(None, "prow", None, None, "pcol", None), P())
    return jax.shard_map(
        shards,
        mesh=mesh,
        in_specs=placed,
        out_specs=P(None, "prow", None, None, "pcol", None),
        check_vma=False,
    )
```

profile of v0, /device:TPU:50, one launch (start us, length us, event | category | flops | bytes accessed | tf_op | source)
XLA Modules:
  0.0 118.2 jit_solution(557761095181068410)
XLA Ops:
  6.5 2.2 %indices.1 = (s32[16,256]{1,0:T(8,128)S(1)}, s32[256,128]{1,0:T(8,128)S(1)}) custom-call(s32[2,128]{1,0:T(2,128)} %piv_ref.1), custom_call_target="tpu_custom_call" | custom-call | tf_op jit(solution)/shard_map/indices/pallas_call | solution.py:292
  8.7 0.5 slice.57
  9.9 69.7 %conditional.1 = (f32[4608,128]{1,0:T(8,128)}, f32[3072,128]{1,0:T(8,128)}, f32[2,2688,128]{2,1,0:T(8,128)}, s32[16,256]{1,0:T(8,128)S(1)}, s32[256,128]{1,0:T(8,128)S(1)}) conditional(s32[]{:T(128)} %bitcast.9, (s32[16,256]{1,0:T(8,128)S(1)}, s32[]{:T(128)}, f32[16,1,128,12,1,128]{5,4,3,2,1,0:T(1,128)}, s32[]{:T(128)}) %tuple.21, ...), branch_computations={%region_0.4_spmd, %region_4.5_spmd} | conditional | flops 5115396 | bytes 127421608 | solution.py:738
  9.9 6.0 %gather.7 = (f32[1152,128]{1,0:T(8,128)S(1)}, f32[3072,128]{1,0:T(8,128)S(1)}, f32[96,128]{1,0:T(8,128)S(1)}, f32[256,128]{1,0:T(8,128)S(1)}, f32[2048,128]{1,0:T(8,128)S(1)}) custom-call(s32[16,256]{1,0:T(8,128)S(1)} %get-tuple-element.98.idx_ref, f32[24576,128]{1,0:T(8,128)} %get-tuple-element.48.x_ref), custom_call_target="tpu_custom_call" | custom-call | tf_op jit(solution)/shard_map/cond/branch_1_fun/gather/pallas_call | solution.py:338
  15.9 0.0 copy-start
  15.9 1.1 copy-done
  17.1 0.0 copy-start.1
  17.1 1.0 copy-done.1
  18.0 0.0 copy-start.2
  18.0 0.9 copy-done.2
  18.9 0.0 copy-start.3
  18.9 0.6 copy-done.3
  19.6 0.0 copy-start.4
  19.6 0.6 copy-done.4
  20.2 59.2 %exchange.1 = (f32[4608,128]{1,0:T(8,128)}, f32[3072,128]{1,0:T(8,128)}, f32[2,2688,128]{2,1,0:T(8,128)}, f32[768,128]{1,0:T(8,128)}) custom-call(f32[1152,128]{1,0:T(8,128)} %copy-done.2, f32[3072,128]{1,0:T(8,128)} %copy-done, f32[96,128]{1,0:T(8,128)} %copy-done.4, f32[256,128]{1,0:T(8,128)} %copy-done.3, f32[2048,128]{1,0:T(8,128)} %copy-done.1), custom_call_target="tpu_custom_call" | custom-call | tf_op jit(solution)/shard_map/cond/branch_1_fun/exchange/pallas_call | solution.py:606
  79.6 0.0 copy-start.5
  79.6 14.7 %factor.1 = (f32[256,256]{1,0:T(8,128)S(1)}, f32[256,256]{1,0:T(8,128)S(1)}, f32[256,256]{1,0:T(8,128)S(1)}) custom-call(f32[2,2688,128]{2,1,0:T(8,128)} %get-tuple-element.71.arr_ref.panel_ref, s32[256,128]{1,0:T(8,128)S(1)} %get-tuple-element.74.slot_ref), custom_call_target="tpu_custom_call" | custom-call | tf_op jit(solution)/shard_map/factor/pallas_call | solution.py:161
  94.3 0.0 copy-done.5
  94.3 17.0 %update.1 = f32[24576,128]{1,0:T(8,128)} custom-call(s32[16,256]{1,0:T(8,128)S(1)} %get-tuple-element.70.idx_ref, f32[24576,128]{1,0:T(8,128)} %bitcast.17, f32[2,2688,128]{2,1,0:T(8,128)S(1)} %copy-done.5, f32[3072,128]{1,0:T(8,128)} %get-tuple-element.72.disp_ref, f32[4608,128]{1,0:T(8,128)} %get-tuple-element.73.arr_ref, ...), custom_call_target="tpu_custom_call" | custom-call | tf_op jit(solution)/shard_map/update/pallas_call | solution.py:694
Async XLA Ops:
  15.9 1.1 copy-start
  17.1 1.0 copy-start.1
  18.0 0.9 copy-start.2
  18.9 0.6 copy-start.3
  19.6 0.6 copy-start.4
  79.6 14.7 %copy-start.5 = (f32[2,2688,128]{2,1,0:T(8,128)S(1)}, f32[2,2688,128]{2,1,0:T(8,128)}, u32[]{:S(2)}) copy-start(f32[2,2688,128]{2,1,0:T(8,128)} %get-tuple-element.71.arr_ref.panel_ref) | copy-start | bytes 8257540
where the time goes:
time: 118 us
  Pallas kernels  99.1 us (84%)
  between operations  14.1 us (12%)
  local copies, waits for them, and re-layouts  4.74 us (4%)
    pallas_call x1, Pallas kernels, exchange_call(): pl.pallas_call(exchange_kernel, in_specs=[pl.BlockSpec(memory_space=pltpu...  59.2 us
    pallas_call x1, Pallas kernels, update_call(): pl.pallas_call(update_kernel, grid=(16 * NB // STEP_ROWS,), in_specs=[pl....  17 us
    pallas_call x1, Pallas kernels, lu_call(): pl.pallas_call(lu_kernel, grid=(1,), in_specs=[pl.BlockSpec((2, 4 * SLOTS...  14.7 us
    pallas_call x1, Pallas kernels, gather_call(): pl.pallas_call(gather_kernel, in_specs=[pl.BlockSpec(memory_space=pltpu.S...  6.03 us
    cond x10, local copies, waits for them, and re-layouts  4.23 us

commit v1 on v0

--- a/solution.py
+++ b/solution.py
@@ -11,11 +11,11 @@
 MESH = pl.DeviceIdType.MESH
 SLOTS_A = 96
 SLOTS_D = 64
-LOADS = 8
+LOADS = 16
+PIECE = NB + 16
 (
-    OWNER, LOCAL, OVER, ARR_LOCAL, ARR_COUNT, OUT_LOCAL, OUT_SLOT, OUT_COUNT,
-    IN_TARGET, IN_ROW, IN_LINE, IN_ORIGIN, IN_COUNT,
-) = range(13)
+    OWNER, LOCAL, OVER, ARR_LOCAL, OUT_LOCAL, IN_TARGET, IN_ROW, IN_LINE, IN_ORIGIN, IN_COUNT,
+) = range(10)
 
 
 def split(x):
@@ -116,13 +116,7 @@
         t_ref[1, pl.ds(local, 16), :] = zero
 
 
-def lu_core(a_ref, xl_ref, xu_ref, t_ref):
-    t_ref[...] = jnp.zeros(t_ref.shape, F32)
-    for half in range(2):
-        def step(index, carry, half=half):
-            eliminate(a_ref, xl_ref, xu_ref, t_ref, index, half)
-            return carry
-        lax.fori_loop(0, 8, step, 0)
+def inverses(a_ref, xl_ref, xu_ref):
     packed = jnp.concatenate([a_ref[0], a_ref[1]], 1)
     left = jnp.concatenate([xl_ref[0], xl_ref[1]], 1)
     right = jnp.concatenate([xu_ref[0], xu_ref[1]], 1)
@@ -143,34 +137,34 @@
     return packed, left, right
 
 
-def lu_kernel(arr_ref, slot_ref, packed_ref, linv_ref, uinv_ref, a_ref, xl_ref, xu_ref, t_ref):
-    count = arr_ref.shape[1]
-    slot = slot_ref[:, :1]
-    onehot = jnp.where(iota((256, count), 1) == slot, 1.0, 0.0).astype(BF16)
+def lu_kernel(square_ref, packed_ref, linv_ref, uinv_ref, a_ref, xl_ref, xu_ref, t_ref):
+    a_ref[...] = square_ref[...]
+    t_ref[...] = jnp.zeros(t_ref.shape, F32)
     for half in range(2):
-        a_ref[half] = onehot_rows(onehot, arr_ref[half])
-    packed, left, right = lu_core(a_ref, xl_ref, xu_ref, t_ref)
+        def step(index, carry, half=half):
+            eliminate(a_ref, xl_ref, xu_ref, t_ref, index, half)
+            return carry
+
+        lax.fori_loop(0, 8, step, 0)
+    packed, left, right = inverses(a_ref, xl_ref, xu_ref)
     packed_ref[...] = packed
     linv_ref[...] = left
     uinv_ref[...] = right
 
 
-def lu_call(arr, slot_col):
-    square = jax.ShapeDtypeStruct((256, 256), F32)
-    whole = pl.BlockSpec((256, 256), lambda i: (0, 0))
+def lu_call(square):
+    result = jax.ShapeDtypeStruct((2 * NB, 2 * NB), F32)
     return pl.pallas_call(
         lu_kernel,
-        grid=(1,),
-        in_specs=[
-            pl.BlockSpec((2, 4 * SLOTS_A, NB), lambda i: (0, 0, 0)),
-            pl.BlockSpec((256, NB), lambda i: (0, 0)),
-        ],
-        out_specs=[whole] * 3,
-        out_shape=[square] * 3,
-        scratch_shapes=[pltpu.VMEM((2, 256, 128), F32)] * 3 + [pltpu.VMEM((2, 128, 128), F32)],
+        out_shape=[result] * 3,
+        scratch_shapes=[pltpu.VMEM((2, 2 * NB, NB), F32)] * 3 + [pltpu.VMEM((2, NB, NB), F32)],
         compiler_params=pltpu.CompilerParams(vmem_limit_bytes=32 * 2**20),
         name="factor",
-    )(arr, slot_col)
+    )(square)
+
+
+def panel_line(number):
+    return (number >> 4) * PIECE + NB + (number & 15)
 
 
 def index_kernel(piv_ref, idx_ref, slot_ref):
@@ -258,25 +252,26 @@
         count = whole(total + subs_sum(chosen_col[1] > 0.0))
         return packed, [count, count]
 
-    (arr_local,), arr_count = compact([o == me for o in owners], [locals_])
-    (out_local, out_slot), out_count = compact(
-        [v & (h == me) for v, h in zip(valid, halves)],
-        [
-            [x & (NB - 1) for x in origins],
-            [d * SLOTS_D + r for d, r in zip(dests, rank_disp)],
-        ],
-    )
+    (arr_local,), _ = compact([o == me for o in owners], [locals_])
+    out_slot = [
+        jnp.where(v & (h == me), d * SLOTS_D + r, -1).astype(F32).T
+        for v, h, d, r in zip(valid, halves, dests, rank_disp)
+    ]
+    out_row = [(x & (NB - 1)).astype(F32).T for x in origins]
+    out_local = [
+        whole(sum(subs_sum(o == lane + g * NB, v) for o, v in zip(out_slot, out_row))) for g in range(2)
+    ]
     (in_target, in_row, in_line, in_origin), in_count = compact(
         [v & (d == me) for v, d in zip(valid, dests)],
         [
             targets,
             [h * NB + r for h, r in zip(halves, rank_disp)],
-            [h * SLOTS_D + r for h, r in zip(halves, rank_disp)],
+            [panel_line(h * SLOTS_D + r) for h, r in zip(halves, rank_disp)],
             origins,
         ],
     )
     fields = [
-        owners, locals_, [over, over], arr_local, arr_count, out_local, out_slot, out_count,
+        owners, locals_, [over, over], arr_local, out_local,
         in_target, in_row, in_line, in_origin, in_count,
     ]
     for number, field in enumerate(fields):
@@ -299,125 +294,95 @@
     )(pivots)
 
 
-def gather_kernel(idx_ref, x_ref, arr_ref, disp_ref, arr_line_ref, disp_line_ref, raw_ref, whole, sems):
-    me = lax.axis_index("prow")
+ANY = pl.BlockSpec(memory_space=pl.ANY)
+
+
+def rows8(start, size):
+    return pl.ds(pl.multiple_of(start, 8), size)
+
+
+def front_kernel(
+    idx_ref, slot_ref, x_ref, recv_arr, recv_disp, panel, packed_ref, linv_ref, uinv_ref,
+    whole, top, arr_ref, disp_ref, arr_line_ref, disp_line_ref, raw_ref, arr_buf, disp_buf, square,
+    a_ref, xl_ref, xu_ref, t_ref,
+    load_sem, local_sem, y_send, y_recv, p_send, p_recv, t_send, t_recv, s_send, s_recv,
+    scatter_send, scatter_recv, x_send, x_recv, z_send, z_recv, pair_send, pair_recv,
+):
     lines = whole.shape[0] // (16 * NB)
-    part = whole.shape[0] // LOADS
+    size = whole.shape[0] // LOADS
+    load_top = pltpu.make_async_copy(x_ref.at[pl.ds(0, NB * lines)], top, local_sem.at[5])
+    load_top.start()
     loads = []
     for number in range(LOADS):
-        here = pl.ds(number * part, part)
-        loads.append(pltpu.make_async_copy(x_ref.at[here], whole.at[here], sems.at[number]))
+        here = pl.ds(number * size, size)
+        loads.append(pltpu.make_async_copy(x_ref.at[here], whole.at[here], load_sem.at[number]))
         loads[-1].start()
-    arr_ref[...] = jnp.zeros(arr_ref.shape, F32)
-    for load in loads:
-        load.wait()
-
-    def arriving(j, carry):
-        arr_ref[pl.ds(j * lines, lines), :] = whole[pl.ds(idx_ref[ARR_LOCAL, j] * lines, lines), :]
-        return carry
-
-    def displaced(t, carry):
-        disp_ref[pl.ds(idx_ref[OUT_SLOT, t] * lines, lines), :] = whole[
-            pl.ds(idx_ref[OUT_LOCAL, t] * lines, lines), :
-        ]
-        return carry
-
-    lax.fori_loop(0, idx_ref[ARR_COUNT, 0], arriving, 0)
-    lax.fori_loop(0, idx_ref[OUT_COUNT, 0], displaced, 0)
-    arr_line_ref[...] = arr_ref[pl.ds(0, SLOTS_A, lines), :]
-    disp_line_ref[...] = disp_ref[pl.ds(0, 4 * SLOTS_D, lines), :]
-    raw_ref[...] = whole[pl.ds(0, 16 * NB, lines), :]
-
-
-ANY = pl.BlockSpec(memory_space=pl.ANY)
-
-
-def gather_call(idx, x, lines):
-    sizes = [SLOTS_A * lines, 4 * SLOTS_D * lines, SLOTS_A, 4 * SLOTS_D, 16 * NB]
-    vmem = pl.BlockSpec(memory_space=pltpu.VMEM)
-    return pl.pallas_call(
-        gather_kernel,
-        in_specs=[pl.BlockSpec(memory_space=pltpu.SMEM), ANY],
-        out_specs=[vmem] * 5,
-        out_shape=[jax.ShapeDtypeStruct((size, NB), F32) for size in sizes],
-        scratch_shapes=[pltpu.VMEM(x.shape, F32), pltpu.SemaphoreType.DMA((LOADS,))],
-        compiler_params=pltpu.CompilerParams(vmem_limit_bytes=40 * 2**20),
-        name="gather",
-    )(idx, x)
-
-
-DISP_LINES = 4 * SLOTS_A
-RAW_LINES = DISP_LINES + 2 * NB
-TREE_BLOCKS = 5
-
-
-def rows8(start, size):
-    return pl.ds(pl.multiple_of(start, 8), size)
-
-
-def exchange_kernel(
-    arr_ref, disp_ref, arr_line_ref, disp_line_ref, raw_ref, recv_arr, recv_disp, panel, relay,
-    local_sem, y_send, y_recv, p_send, p_recv, t_send, t_recv, s_send, s_recv,
-):
     p = lax.axis_index("prow")
     q = lax.axis_index("pcol")
     cx, cz, core = q // 8, (q // 2) % 4, q % 2
     root = q < 2
 
     def column(ix, iz, icore):
-        return ((ix + 4) % 4 * 4 + (iz + 4) % 4) * 2 + icore
+        return (ix % 4 * 4 + iz % 4) * 2 + icore
 
     up, down, across = ((p + 1) % 4, q), ((p + 3) % 4, q), ((p + 2) % 4, q)
     sibling = (p, column(cx, cz, 1 - core))
-    near = [
-        up, down, across, sibling,
-        (p, column(cx + 1, cz, core)), (p, column(cx + 3, cz, core)),
-        (p, column(cx, cz + 1, core)), (p, column(cx, cz + 3, core)),
-    ]
+    x_peers = [(p, column(cx + i, cz, core)) for i in (1, 2, 3)]
+    z_peers = [(p, column(cx, cz + i, core)) for i in (1, 2, 3)]
+    near = [up, down, across, sibling] + x_peers + z_peers
     barrier = pltpu.get_barrier_semaphore()
     for other in near:
         pl.semaphore_signal(barrier, inc=1, device_id=other, device_id_type=MESH)
-    pl.semaphore_wait(barrier, len(near))
+
+    @pl.when((cx > 0) & (cz > 0))
+    def _():
+        pl.semaphore_signal(barrier, inc=1, device_id=(p, core), device_id_type=MESH)
 
     def remote(src, dst, send, recv, device):
         return pltpu.make_async_remote_copy(
             src_ref=src, dst_ref=dst, send_sem=send, recv_sem=recv, device_id=device, device_id_type=MESH
         )
 
+    load_top.wait()
+
+    def displaced(t, carry):
+        disp_ref[pl.ds(t * lines, lines), :] = top[pl.ds(idx_ref[OUT_LOCAL, t] * lines, lines), :]
+        return carry
+
+    def arriving(j, carry):
+        arr_ref[pl.ds(j * lines, lines), :] = whole[pl.ds(idx_ref[ARR_LOCAL, j] * lines, lines), :]
+        return carry
+
+    @pl.when(p < 2)
+    def _():
+        lax.fori_loop(0, 4 * SLOTS_D, displaced, 0, unroll=4)
+        disp_line_ref[...] = disp_ref[pl.ds(0, 4 * SLOTS_D, lines), :]
+
+    pl.semaphore_wait(barrier, jnp.where(root, len(near) + 9, len(near)))
+
     def arr_lines(owner):
-        return panel.at[core, rows8(owner * SLOTS_A, SLOTS_A)]
+        return arr_buf.at[rows8(owner * SLOTS_A, SLOTS_A)]
 
     def disp_lines(half):
-        return panel.at[core, rows8(DISP_LINES + half * SLOTS_D, SLOTS_D)]
+        return disp_buf.at[rows8(half * SLOTS_D, SLOTS_D)]
 
     def disp_for(owner):
         return disp_line_ref.at[rows8(owner * SLOTS_D, SLOTS_D)]
 
     peers = [up, down, across]
-    own_raw = pltpu.make_async_copy(raw_ref, panel.at[core, pl.ds(RAW_LINES, 16 * NB)], local_sem.at[0])
     own_arr = pltpu.make_async_copy(arr_line_ref, arr_lines(p), local_sem.at[1])
     own_disp = pltpu.make_async_copy(disp_for(p), disp_lines(p % 2), local_sem.at[2])
-    arr_panel = [
-        remote(arr_line_ref, arr_lines(p), p_send.at[i], p_recv.at[i], peers[i]) for i in range(3)
-    ]
+    arr_panel = [remote(arr_line_ref, arr_lines(p), p_send.at[i], p_recv.at[i], peers[i]) for i in range(3)]
     disp_panel = [
         remote(disp_for(peers[i][0]), disp_lines(p % 2), p_send.at[3 + i], p_recv.at[3 + p % 2], peers[i])
         for i in range(3)
     ]
 
-    @pl.when(root)
-    def _():
-        for copy in arr_panel:
+    @pl.when(root & (p < 2))
+    def _():
+        for copy in disp_panel:
             copy.start()
-
-        @pl.when(p < 2)
-        def _():
-            for copy in disp_panel:
-                copy.start()
-            own_disp.start()
-
-        own_arr.start()
-        own_raw.start()
+        own_disp.start()
 
     arr_size, disp_size = arr_ref.shape[0], disp_ref.shape[0] // 4
     half_size = arr_size // 2
@@ -440,86 +405,97 @@
         remote(arr_ref.at[high], arr_rows(p, high), y_send.at[2], y_recv.at[2], up),
         remote(arr_ref.at[low], arr_rows(p, low), y_send.at[3], y_recv.at[3], down),
     ]
-    for copy in bulk:
-        copy.start()
-    own_rows.start()
-
     half = p % 2
     to_up = remote(moved_to(up[0]), moved(half), y_send.at[4], y_recv.at[4 + half], up)
     to_down = remote(moved_to(down[0]), moved(half), y_send.at[5], y_recv.at[4 + half], down)
-    via = [
-        remote(moved_to(2), relay, y_send.at[6], y_recv.at[6], down),
-        remote(moved_to(3), relay, y_send.at[6], y_recv.at[6], up),
-    ]
+    to_across = remote(moved_to(across[0]), moved(half), y_send.at[6], y_recv.at[4 + half], across)
 
     @pl.when(p < 2)
     def _():
-        to_up.start()
-        to_down.start()
+        to_across.start()
         own_moved.start()
-
-    for number in range(2):
-        @pl.when(p == number)
-        def _(number=number):
-            via[number].start()
 
     forward = [
         remote(arr_rows(down[0], low), arr_rows(down[0], low), y_send.at[7], y_recv.at[7], up),
         remote(arr_rows(up[0], high), arr_rows(up[0], high), y_send.at[8], y_recv.at[8], down),
     ]
-
-    def block(which, stream, k):
-        line = jnp.where(k == 0, stream * NB, RAW_LINES + (stream * (TREE_BLOCKS - 1) + k - 1) * NB)
-        return panel.at[which, pl.ds(pl.multiple_of(line, NB), NB)]
-
-    def along(stream):
-        sign = 1 if stream % 2 == 0 else 3
-        return sign, (cx * sign) % 4, (cz * sign) % 4
-
-    def tree(stream, k):
-        sign, ax, az = along(stream)
-        next_x = (p, column(cx + sign, cz, core))
-        next_z = (p, column(cx, cz + sign, core))
-        first, second = (ax, az) if stream < 2 else (az, ax)
-        to_first, to_second = (next_x, next_z) if stream < 2 else (next_z, next_x)
-        number = stream * TREE_BLOCKS + k
-        ref = block(core, stream, k)
-        return (
-            (second == 0) & (first < 3),
-            remote(ref, ref, t_send.at[0, number], t_recv.at[number], to_first),
-            second < 3,
-            remote(ref, ref, t_send.at[1, number], t_recv.at[number], to_second),
-            remote(ref, ref, s_send.at[number], s_recv.at[number], sibling),
+    for load in loads:
+        load.wait()
+    lax.fori_loop(0, SLOTS_A, arriving, 0, unroll=4)
+    arr_line_ref[...] = arr_ref[pl.ds(0, SLOTS_A, lines), :]
+
+    @pl.when(root)
+    def _():
+        for copy in arr_panel:
+            copy.start()
+        own_arr.start()
+
+    for copy in bulk[:2]:
+        copy.start()
+    own_rows.start()
+
+    upper, lower = square.at[core, pl.ds(0, NB)], square.at[core, pl.ds(NB, NB)]
+    upper_x = [remote(upper, upper, t_send.at[0, i], t_recv.at[0], x_peers[i]) for i in range(3)]
+    lower_z = [remote(lower, lower, t_send.at[1, i], t_recv.at[1], z_peers[i]) for i in range(3)]
+    upper_z = [remote(upper, upper, t_send.at[2, i], t_recv.at[0], z_peers[i]) for i in range(3)]
+    lower_x = [remote(lower, lower, t_send.at[3, i], t_recv.at[1], x_peers[i]) for i in range(3)]
+    own_square = remote(square.at[core], square.at[core], s_send.at[0], s_recv.at[0], sibling)
+
+    start, end = pl.ds(0, PIECE // 2), pl.ds(PIECE // 2, PIECE // 2)
+    scatter = [
+        remote(
+            raw_ref.at[i], panel.at[core, i // 4, i % 4], scatter_send.at[i - 1], scatter_recv.at[0],
+            (p, column(i // 4, i % 4, core)),
         )
-
-    def pass_on(stream, step):
-        _, ax, az = along(stream)
-        depth = ax + az
-        k = step - depth
-
-        @pl.when((k >= 0) & (k < TREE_BLOCKS))
-        def _():
-            go_first, send_first, go_second, send_second, send_sibling = tree(stream, k)
-
-            @pl.when(depth > 0)
-            def _():
-                send_first.wait_recv()
-
-            @pl.when(go_first)
-            def _():
-                send_first.start()
-
-            @pl.when(go_second)
-            def _():
-                send_second.start()
-
-            send_sibling.start()
+        for i in range(1, 16)
+    ]
+    own_piece = pltpu.make_async_copy(raw_ref.at[0], panel.at[core, 0, 0], local_sem.at[0])
+    along = []
+    for i in range(3):
+        mine_low, mine_high = panel.at[core, cx, cz, start], panel.at[core, cx, cz, end]
+        along.append(remote(mine_low, mine_low, x_send.at[0, i], x_recv.at[0, i], x_peers[i]))
+        along.append(remote(mine_high, mine_high, z_send.at[0, i], z_recv.at[0, i], z_peers[i]))
+    spread = []
+    for i in range(3):
+        mine_low, mine_high = panel.at[core, :, cz, start], panel.at[core, cx, :, end]
+        spread.append(remote(mine_low, mine_low, z_send.at[1, i], z_recv.at[1, i], z_peers[i]))
+        spread.append(remote(mine_high, mine_high, x_send.at[1, i], x_recv.at[1, i], x_peers[i]))
+    pair = remote(panel.at[core], panel.at[core], pair_send.at[0], pair_recv.at[0], sibling)
 
     @pl.when(root)
     def _():
+        for i in range(16):
+            raw_ref[i, :NB] = whole[pl.ds(i * NB * lines, NB, lines), :]
         own_arr.wait()
         for copy in arr_panel:
             copy.wait_recv()
+        onehot = jnp.where(iota((2 * NB, 4 * SLOTS_A), 1) == slot_ref[:, :1], 1.0, 0.0).astype(BF16)
+        square[core] = onehot_rows(onehot, arr_buf[...])
+        for copy in upper_x + lower_z:
+            copy.start()
+
+    @pl.when(jnp.logical_not(root))
+    def _():
+        upper_x[0].wait_recv()
+
+    @pl.when(cz == 0)
+    def _():
+        for copy in upper_z:
+            copy.start()
+
+    @pl.when(jnp.logical_not(root))
+    def _():
+        lower_z[0].wait_recv()
+
+    @pl.when(cx == 0)
+    def _():
+        for copy in lower_x:
+            copy.start()
+
+    own_square.start()
+
+    @pl.when(root)
+    def _():
         for source in range(2):
             @pl.when(p == source)
             def _():
@@ -528,27 +504,67 @@
             @pl.when(p != source)
             def _(source=source):
                 remote(disp_for(0), disp_lines(source), p_send.at[3], p_recv.at[3 + source], up).wait_recv()
-        own_raw.wait()
-
-    def tree_step(step, carry):
-        for stream in range(4):
-            pass_on(stream, step)
-        return carry
-
-    lax.fori_loop(0, 6, tree_step, 0)
-    bulk[0].wait_recv()
-    forward[0].start()
-    bulk[1].wait_recv()
-    forward[1].start()
-    lax.fori_loop(6, 6 + TREE_BLOCKS, tree_step, 0)
-    for number in range(2):
-        @pl.when(p == 3 - number)
-        def _(number=number):
-            target = (2, q) if number == 0 else (3, q)
-            remote(relay, relay, y_send.at[6], y_recv.at[6], target).wait_recv()
-            onward = remote(relay, moved(number), y_send.at[9], y_recv.at[4 + number], target)
-            onward.start()
-            onward.wait_send()
+        for i in range(16):
+            raw_ref[i, NB:] = disp_buf[i * 16 : i * 16 + 16, :] if i * 16 < 2 * SLOTS_D else jnp.zeros((16, NB), F32)
+        for copy in scatter:
+            copy.start()
+        own_piece.start()
+
+    for copy in bulk[2:]:
+        copy.start()
+
+    @pl.when(p < 2)
+    def _():
+        to_up.start()
+        to_down.start()
+
+    own_square.wait_recv()
+    a_ref[...] = square[...]
+    t_ref[...] = jnp.zeros(t_ref.shape, F32)
+
+    def pass_rows():
+        bulk[0].wait_recv()
+        forward[0].start()
+        bulk[1].wait_recv()
+        forward[1].start()
+
+    def pass_piece():
+        @pl.when(root)
+        def _():
+            own_piece.wait()
+
+        @pl.when(jnp.logical_not(root))
+        def _():
+            scatter[0].wait_recv()
+
+        for copy in along:
+            copy.start()
+
+    def pass_pieces():
+        for copy in along:
+            copy.wait_recv()
+        for copy in spread:
+            copy.start()
+
+    def pass_panel():
+        for copy in spread:
+            copy.wait_recv()
+        pair.start()
+
+    events = [{2: pass_piece, 3: pass_rows, 6: pass_pieces}, {6: pass_panel}]
+    for half_number in range(2):
+        def factor_step(index, carry, half_number=half_number):
+            for when, event in events[half_number].items():
+                pl.when(index == when)(event)
+            eliminate(a_ref, xl_ref, xu_ref, t_ref, index, half_number)
+            return carry
+
+        lax.fori_loop(0, 8, factor_step, 0)
+    packed, left, right = inverses(a_ref, xl_ref, xu_ref)
+    packed_ref[...] = packed
+    linv_ref[...] = left
+    uinv_ref[...] = right
+
     bulk[2].wait_recv()
     bulk[3].wait_recv()
     for copy in forward:
@@ -562,36 +578,31 @@
         @pl.when(p != source)
         def _(source=source):
             remote(moved_to(0), moved(source), y_send.at[4], y_recv.at[4 + source], up).wait_recv()
-    for copy in bulk + forward:
+    pair.wait_recv()
+    for copy in bulk + forward + along + spread + [pair]:
         copy.wait_send()
 
     @pl.when(p < 2)
     def _():
         to_up.wait_send()
         to_down.wait_send()
-        via[0].wait_send()
-
-    def finish(k, carry):
-        for stream in range(4):
-            go_first, send_first, go_second, send_second, send_sibling = tree(stream, k)
-
-            @pl.when(go_first)
-            def _():
-                send_first.wait_send()
-
-            @pl.when(go_second)
-            def _():
-                send_second.wait_send()
-
-            send_sibling.wait_send()
-            send_sibling.wait_recv()
-        return carry
-
-    lax.fori_loop(0, TREE_BLOCKS, finish, 0)
+        to_across.wait_send()
+
+    @pl.when(cz == 0)
+    def _():
+        for copy in upper_z:
+            copy.wait_send()
+
+    @pl.when(cx == 0)
+    def _():
+        for copy in lower_x:
+            copy.wait_send()
+
+    own_square.wait_send()
 
     @pl.when(root)
     def _():
-        for copy in arr_panel:
+        for copy in arr_panel + upper_x + lower_z + scatter:
             copy.wait_send()
 
         @pl.when(p < 2)
@@ -600,20 +611,30 @@
                 copy.wait_send()
 
 
-def exchange_call(operands, lines):
+def front_call(idx, slot, x, lines):
     dma = pltpu.SemaphoreType.DMA
-    sizes = [(4 * SLOTS_A * lines,), (2 * NB * lines,), (2, RAW_LINES + 16 * NB), (SLOTS_D * lines,)]
+    vmem = pl.BlockSpec(memory_space=pltpu.VMEM)
+    result = jax.ShapeDtypeStruct((2 * NB, 2 * NB), F32)
+    sizes = [(4 * SLOTS_A * lines,), (2 * NB * lines,), (2, 4, 4, PIECE)]
+    held = [
+        x.shape[:1], (NB * lines,), (SLOTS_A * lines,), (4 * SLOTS_D * lines,), (SLOTS_A,), (4 * SLOTS_D,), (16, PIECE),
+        (4 * SLOTS_A,), (2 * SLOTS_D,), (2, 2 * NB), (2, 2 * NB), (2, 2 * NB), (2, 2 * NB), (2, NB),
+    ]
+    semaphores = [
+        (LOADS,), (6,), (9,), (9,), (6,), (5,), (4, 3), (2,), (1,), (1,),
+        (15,), (1,), (2, 3), (2, 3), (2, 3), (2, 3), (1,), (1,),
+    ]
     return pl.pallas_call(
-        exchange_kernel,
-        in_specs=[pl.BlockSpec(memory_space=pltpu.VMEM)] * 5,
-        out_specs=[ANY] * 4,
-        out_shape=[jax.ShapeDtypeStruct(size + (NB,), F32) for size in sizes],
-        scratch_shapes=[
-            dma((5,)), dma((10,)), dma((9,)), dma((6,)), dma((5,)), dma((2, 20)), dma((20,)), dma((20,)), dma((20,)),
-        ],
-        compiler_params=pltpu.CompilerParams(collective_id=0, has_side_effects=True),
-        name="exchange",
-    )(*operands)
+        front_kernel,
+        in_specs=[pl.BlockSpec(memory_space=pltpu.SMEM), vmem, ANY],
+        out_specs=[ANY] * 3 + [vmem] * 3,
+        out_shape=[jax.ShapeDtypeStruct(size + (NB,), F32) for size in sizes] + [result] * 3,
+        scratch_shapes=[pltpu.VMEM(size + (NB,), F32) for size in held] + [dma(shape) for shape in semaphores],
+        compiler_params=pltpu.CompilerParams(
+            collective_id=0, has_side_effects=True, vmem_limit_bytes=48 * 2**20
+        ),
+        name="front",
+    )(idx, slot, x)
 
 
 STEP_ROWS = 256
@@ -652,17 +673,21 @@
 
         def patch(t, carry):
             target = idx_ref[IN_TARGET, t]
-            line = idx_ref[IN_LINE, t] + DISP_LINES
+            line = idx_ref[IN_LINE, t]
+            panel_row = (target >> 7) * PIECE + (target & (NB - 1))
             for half in range(2):
-                pan[half, pl.ds(RAW_LINES + target, 1), :] = pan[half, pl.ds(line, 1), :]
+                pan[half, pl.ds(panel_row, 1), :] = pan[half, pl.ds(line, 1), :]
             source = idx_ref[IN_ROW, t] * lines
             whole[pl.ds(target * lines, lines), :] = disp_ref[pl.ds(source, lines), :]
             return carry
 
         lax.fori_loop(0, idx_ref[IN_COUNT, 0], patch, 0)
 
-    here = pl.ds(pl.multiple_of(RAW_LINES + step * STEP_ROWS, NB), STEP_ROWS)
-    rows = jnp.concatenate([pan[0, here, :], pan[1, here, :]], 1)
+    rows = []
+    for number in range(STEP_ROWS // NB):
+        here = pl.ds(pl.multiple_of((step * (STEP_ROWS // NB) + number) * PIECE, 8), NB)
+        rows.append(jnp.concatenate([pan[0, here, :], pan[1, here, :]], 1))
+    rows = jnp.concatenate(rows, 0)
     mult = dot3(split(rows), split(uinv_ref[...]))
     high, low = split(mult)
     left = jnp.concatenate([high, high, low], 1)
@@ -699,7 +724,7 @@
         out_shape=jax.ShapeDtypeStruct((16 * NB * lines, NB), F32),
         scratch_shapes=[
             pltpu.VMEM((16 * NB * lines, NB), F32),
-            pltpu.VMEM((2, RAW_LINES + 16 * NB, NB), F32),
+            pltpu.VMEM((2, 16 * PIECE, NB), F32),
             pltpu.VMEM((6 * NB, NB * lines), BF16),
             pltpu.VMEM((2 * NB, NB * lines), F32),
             pltpu.SemaphoreType.DMA,
@@ -718,25 +743,35 @@
     x = matrix.reshape(rows * lines, NB)
     idx, slot = index_call(pivots)
 
+    def total(x, axis, count):
+        bit = 1
+        while bit < count:
+            x = x + lax.ppermute(x, axis, [(i, i ^ bit) for i in range(count)])
+            bit *= 2
+        return x
+
     def fits(x, idx, slot):
-        recv_arr, recv_disp, panel, _ = exchange_call(gather_call(idx, x, lines), lines)
-        return recv_arr, recv_disp, panel, idx, slot
+        recv_arr, recv_disp, panel, packed, linv, uinv = front_call(idx, slot, x, lines)
+        return recv_arr, recv_disp, panel, packed, linv, uinv, idx, slot
 
     def general(x, idx, slot):
         x = x.reshape(rows, lines, NB)
         chosen = jnp.where((idx[OWNER] == p)[:, None, None], jnp.take(x, idx[LOCAL], axis=0), 0.0)
         top = jnp.concatenate([jnp.where(p == s, x[:NB], 0.0) for s in range(2)])
-        chosen, top = lax.psum((chosen, top), "prow")
+        chosen, top = total(chosen, "prow", 4), total(top, "prow", 4)
+        own = jnp.concatenate([x[:, 0].reshape(16, NB, NB), top[:, 0].reshape(16, 16, NB)], 1)
+        own = jnp.concatenate([own.reshape(-1, NB), chosen[:, 0]])
+        both = total(jnp.stack([jnp.where(q == s, own, 0.0) for s in range(2)]), "pcol", 32)
+        panel = both[:, : 16 * PIECE].reshape(2, 4, 4, PIECE, NB)
+        order = jnp.arange(2 * NB, dtype=jnp.int32)
+        idx = idx.at[IN_ROW].set(idx[IN_ORIGIN]).at[IN_LINE].set(panel_line(idx[IN_ORIGIN]))
+        slot = jnp.broadcast_to(order[:, None], slot.shape)
+        packed, linv, uinv = lu_call(both[:, 16 * PIECE :])
         chosen = jnp.pad(chosen, ((0, 4 * SLOTS_A - 2 * NB), (0, 0), (0, 0)))
-        own = jnp.concatenate([chosen[:, 0], top[:, 0], x[:, 0]])
-        panel = lax.psum(jnp.stack([jnp.where(q == s, own, 0.0) for s in range(2)]), "pcol")
-        order = jnp.arange(2 * NB, dtype=jnp.int32)
-        idx = idx.at[IN_ROW].set(idx[IN_ORIGIN]).at[IN_LINE].set(idx[IN_ORIGIN])
-        slot = jnp.broadcast_to(order[:, None], slot.shape)
-        return chosen.reshape(-1, NB), top.reshape(-1, NB), panel, idx, slot
-
-    arr, disp, panel, idx, slot = lax.cond(idx[OVER, 0] == 0, fits, general, x, idx, slot)
-    packed, linv, uinv = lu_call(panel, slot)
+        return chosen.reshape(-1, NB), top.reshape(-1, NB), panel, packed, linv, uinv, idx, slot
+
+    arr, disp, panel, packed, linv, uinv, idx, slot = lax.cond(idx[OVER, 0] == 0, fits, general, x, idx, slot)
+    panel = panel.reshape(2, -1, NB)
     out = update_call(idx, x, panel, disp, arr, slot, packed, linv, uinv, lines)
     return out.reshape(matrix.shape)
 

time: 118 us -> 81.7 us (0.69)
  the two profiles are of different devices: /device:TPU:50 before, /device:TPU:1 now
where the time goes in v1:
time: 81.7 us; the launch traced here: 81.2 us
  Pallas kernels  79.6 us (97%)
  between operations  0.85 us (1%)
    pallas_call x1, Pallas kernels, front_call(): pl.pallas_call(front_kernel, in_specs=[pl.BlockSpec(memory_space=pltpu.SM...  60.3 us
    pallas_call x1, Pallas kernels, update_call(): pl.pallas_call(update_kernel, grid=(16 * NB // STEP_ROWS,), in_specs=[pl....  17.3 us
    pallas_call x1, Pallas kernels, index_call(): pl.pallas_call(index_kernel, out_shape=[jax.ShapeDtypeStruct((16, 2 * NB)...  2.03 us

profile of v1, /device:TPU:1, one launch (start us, length us, event | category | flops | bytes accessed | tf_op | source)
XLA Modules:
  0.0 81.2 jit_solution(6196249456272951085)
XLA Ops:
  0.0 2.0 %indices.1 = (s32[16,256]{1,0:T(8,128)S(1)}, s32[256,128]{1,0:T(8,128)S(1)}) custom-call(s32[2,128]{1,0:T(2,128)} %piv_ref.1), custom_call_target="tpu_custom_call" | custom-call | tf_op jit(solution)/shard_map/indices/pallas_call | solution.py:287
  2.0 0.5 slice.63
  3.2 60.5 %conditional.1 = (f32[4608,128]{1,0:T(8,128)}, f32[3072,128]{1,0:T(8,128)}, f32[256,256]{1,0:T(8,128)S(1)}, f32[256,256]{1,0:T(8,128)S(1)}, f32[256,256]{1,0:T(8...) conditional(s32[]{:T(128)} %bitcast.14, (s32[16,256]{1,0:T(8,128)S(1)}, ...), branch_computations={%region_0.1_spmd, %region_1.0_spmd} | conditional | flops 11506436 | bytes 245257184 | solution.py:773
  3.4 60.3 %front.1 = (f32[4608,128]{1,0:T(8,128)}, f32[3072,128]{1,0:T(8,128)}, f32[2,4,4,144,128]{4,3,2,1,0:T(8,128)S(1)}, f32[256,256]{1,0:T(8,128)S(1)}, f32[256,256]{1,0:T(8,128)S(1)}, /*index=5*/f32[256,256]{1,0:T(8,128)S(1)}) custom-call(s32[16,256]{1,0:T(8,128)S(1)} %get-tuple-element.106.idx_ref, s32[256,128]{1,0:T(8,128)S(1)} %get-tuple-element.107.slot_ref, ...), custom_call_target="tpu_custom_call" | custom-call | tf_op jit(solution)/shard_map/cond/branch_1_fun/front/pallas_call | solution.py:627
  63.7 17.3 %update.1 = f32[24576,128]{1,0:T(8,128)} custom-call(s32[16,256]{1,0:T(8,128)S(1)} %get-tuple-element.72.idx_ref, f32[24576,128]{1,0:T(8,128)} %bitcast.28, f32[2,2304,128]{2,1,0:T(8,128)S(1)} %get-tuple-element.73.panel_ref, f32[3072,128]{1,0:T(8,128)} %get-tuple-element.74.disp_ref, f32[4608,128]{1,0:T(8,128)} %get-tuple-element.75.arr_ref, ...), custom_call_target="tpu_custom_call" | custom-call | tf_op jit(solution)/shard_map/update/pallas_call | solution.py:719

commit v2 on v1

--- a/solution.py
+++ b/solution.py
@@ -9,8 +9,8 @@
 F32 = jnp.float32
 BF16 = jnp.bfloat16
 MESH = pl.DeviceIdType.MESH
-SLOTS_A = 96
-SLOTS_D = 64
+SLOTS_A = 88
+SLOTS_D = 56
 LOADS = 16
 PIECE = NB + 16
 (
@@ -233,13 +233,15 @@
         over = over + whole(rows(jnp.sum(jnp.where(bad, 1.0, 0.0), axis=1, keepdims=True)))
     me = lax.axis_index("prow")
 
-    def compact(chosen, values):
+    def compact(chosen, values, keys):
         chosen = [jnp.where(c, 1.0, 0.0) for c in chosen]
         chosen_col = [c.T for c in chosen]
-        first = subs_sum((chosen_col[0] > 0.0) & (sub < lane))
-        total = subs_sum(chosen_col[0] > 0.0)
-        second = subs_sum((chosen_col[1] > 0.0) & (sub < lane)) + total
-        order = [jnp.where(c > 0.0, r, -1.0).T for c, r in zip(chosen, (first, second))]
+        keys_col = [k.T for k in keys]
+        before = [
+            sum(subs_sum((c > 0.0) & (k < key)) for c, k in zip(chosen_col, keys_col)) for key in keys
+        ]
+        total = sum(subs_sum(c > 0.0) for c in chosen_col)
+        order = [jnp.where(c > 0.0, r, -1.0).T for c, r in zip(chosen, before)]
         packed = []
         for value in values:
             value_col = [v.astype(F32).T for v in value]
@@ -249,10 +251,10 @@
                     for g in range(2)
                 ]
             )
-        count = whole(total + subs_sum(chosen_col[1] > 0.0))
+        count = whole(total)
         return packed, [count, count]
 
-    (arr_local,), _ = compact([o == me for o in owners], [locals_])
+    (arr_local,), _ = compact([o == me for o in owners], [locals_], [lane, lane + NB])
     out_slot = [
         jnp.where(v & (h == me), d * SLOTS_D + r, -1).astype(F32).T
         for v, h, d, r in zip(valid, halves, dests, rank_disp)
@@ -269,6 +271,7 @@
             [panel_line(h * SLOTS_D + r) for h, r in zip(halves, rank_disp)],
             origins,
         ],
+        [t.astype(F32) for t in targets],
     )
     fields = [
         owners, locals_, [over, over], arr_local, out_local,
@@ -430,9 +433,14 @@
             copy.start()
         own_arr.start()
 
-    for copy in bulk[:2]:
+    for copy in bulk:
         copy.start()
     own_rows.start()
+
+    @pl.when(p < 2)
+    def _():
+        to_up.start()
+        to_down.start()
 
     upper, lower = square.at[core, pl.ds(0, NB)], square.at[core, pl.ds(NB, NB)]
     upper_x = [remote(upper, upper, t_send.at[0, i], t_recv.at[0], x_peers[i]) for i in range(3)]
@@ -444,12 +452,22 @@
     start, end = pl.ds(0, PIECE // 2), pl.ds(PIECE // 2, PIECE // 2)
     scatter = [
         remote(
-            raw_ref.at[i], panel.at[core, i // 4, i % 4], scatter_send.at[i - 1], scatter_recv.at[0],
+            raw_ref.at[i], panel.at[core, i // 4, i % 4, pl.ds(0, NB)], scatter_send.at[i - 1], scatter_recv.at[0],
             (p, column(i // 4, i % 4, core)),
         )
         for i in range(1, 16)
     ]
-    own_piece = pltpu.make_async_copy(raw_ref.at[0], panel.at[core, 0, 0], local_sem.at[0])
+    scatter_lines = [
+        remote(
+            disp_buf.at[pl.ds(16 * i, 16)], panel.at[core, i // 4, i % 4, pl.ds(NB, 16)],
+            scatter_send.at[14 + i], scatter_recv.at[1], (p, column(i // 4, i % 4, core)),
+        )
+        for i in range(1, 16)
+    ]
+    own_piece = pltpu.make_async_copy(raw_ref.at[0], panel.at[core, 0, 0, pl.ds(0, NB)], local_sem.at[0])
+    own_lines = pltpu.make_async_copy(
+        disp_buf.at[pl.ds(0, 16)], panel.at[core, 0, 0, pl.ds(NB, 16)], local_sem.at[6]
+    )
     along = []
     for i in range(3):
         mine_low, mine_high = panel.at[core, cx, cz, start], panel.at[core, cx, cz, end]
@@ -465,7 +483,11 @@
     @pl.when(root)
     def _():
         for i in range(16):
-            raw_ref[i, :NB] = whole[pl.ds(i * NB * lines, NB, lines), :]
+            raw_ref[i] = whole[pl.ds(i * NB * lines, NB, lines), :]
+        for copy in scatter:
+            copy.start()
+        own_piece.start()
+        disp_buf[pl.ds(2 * SLOTS_D, 2 * NB - 2 * SLOTS_D), :] = jnp.zeros((2 * NB - 2 * SLOTS_D, NB), F32)
         own_arr.wait()
         for copy in arr_panel:
             copy.wait_recv()
@@ -504,19 +526,9 @@
             @pl.when(p != source)
             def _(source=source):
                 remote(disp_for(0), disp_lines(source), p_send.at[3], p_recv.at[3 + source], up).wait_recv()
-        for i in range(16):
-            raw_ref[i, NB:] = disp_buf[i * 16 : i * 16 + 16, :] if i * 16 < 2 * SLOTS_D else jnp.zeros((16, NB), F32)
-        for copy in scatter:
+        for copy in scatter_lines:
             copy.start()
-        own_piece.start()
-
-    for copy in bulk[2:]:
-        copy.start()
-
-    @pl.when(p < 2)
-    def _():
-        to_up.start()
-        to_down.start()
+        own_lines.start()
 
     own_square.wait_recv()
     a_ref[...] = square[...]
@@ -532,10 +544,12 @@
         @pl.when(root)
         def _():
             own_piece.wait()
+            own_lines.wait()
 
         @pl.when(jnp.logical_not(root))
         def _():
             scatter[0].wait_recv()
+            scatter_lines[0].wait_recv()
 
         for copy in along:
             copy.start()
@@ -602,7 +616,7 @@
 
     @pl.when(root)
     def _():
-        for copy in arr_panel + upper_x + lower_z + scatter:
+        for copy in arr_panel + upper_x + lower_z + scatter + scatter_lines:
             copy.wait_send()
 
         @pl.when(p < 2)
@@ -617,12 +631,12 @@
     result = jax.ShapeDtypeStruct((2 * NB, 2 * NB), F32)
     sizes = [(4 * SLOTS_A * lines,), (2 * NB * lines,), (2, 4, 4, PIECE)]
     held = [
-        x.shape[:1], (NB * lines,), (SLOTS_A * lines,), (4 * SLOTS_D * lines,), (SLOTS_A,), (4 * SLOTS_D,), (16, PIECE),
-        (4 * SLOTS_A,), (2 * SLOTS_D,), (2, 2 * NB), (2, 2 * NB), (2, 2 * NB), (2, 2 * NB), (2, NB),
+        x.shape[:1], (NB * lines,), (SLOTS_A * lines,), (4 * SLOTS_D * lines,), (SLOTS_A,), (4 * SLOTS_D,), (16, NB),
+        (4 * SLOTS_A,), (2 * NB,), (2, 2 * NB), (2, 2 * NB), (2, 2 * NB), (2, 2 * NB), (2, NB),
     ]
     semaphores = [
-        (LOADS,), (6,), (9,), (9,), (6,), (5,), (4, 3), (2,), (1,), (1,),
-        (15,), (1,), (2, 3), (2, 3), (2, 3), (2, 3), (1,), (1,),
+        (LOADS,), (7,), (9,), (9,), (6,), (5,), (4, 3), (2,), (1,), (1,),
+        (30,), (2,), (2, 3), (2, 3), (2, 3), (2, 3), (1,), (1,),
     ]
     return pl.pallas_call(
         front_kernel,
@@ -641,24 +655,41 @@
 
 
 def update_kernel(
-    idx_ref, x_ref, panel_ref, disp_ref, arr_ref, slot_ref, packed_ref, linv_ref, uinv_ref, o_ref,
-    whole, pan, stacked, u_ref, x_sem, pan_sem,
+    idx_ref, x_ref, panel_ref, disp_in, arr_in, slot_ref, packed_ref, linv_ref, uinv_ref, o_ref,
+    whole, pan, disp_ref, arr_ref, stacked, u_ref, done, x_sem, pan_sem, disp_sem, arr_sem,
 ):
     p = lax.axis_index("prow")
     q = lax.axis_index("pcol")
     step = pl.program_id(0)
     lines = whole.shape[0] // (16 * NB)
+    size = STEP_ROWS * lines
+
+    def load_x(number):
+        here = pl.ds(pl.multiple_of(number * size, 8), size)
+        return pltpu.make_async_copy(x_ref.at[here], whole.at[here], x_sem.at[number])
 
     @pl.when(step == 0)
     def _():
-        load = pltpu.make_async_copy(x_ref, whole, x_sem)
-        load.start()
-        load_panel = pltpu.make_async_copy(panel_ref, pan, pan_sem)
-        load_panel.start()
+        loads = []
+        part = 4 * SLOTS_A * lines // 4
+        for number in range(4):
+            here = pl.ds(number * part, part)
+            loads.append(pltpu.make_async_copy(arr_in.at[here], arr_ref.at[here], arr_sem.at[number]))
+        for half in range(2):
+            loads.append(pltpu.make_async_copy(panel_ref.at[half], pan.at[half], pan_sem.at[half]))
+            here = pl.ds(half * NB * lines, NB * lines)
+            loads.append(pltpu.make_async_copy(disp_in.at[here], disp_ref.at[here], disp_sem.at[half]))
+        for load in loads:
+            load.start()
+        for number in range(16 * NB // STEP_ROWS):
+            load_x(number).start()
+        done[0] = 0
         high, low = split(linv_ref[...])
         slot = slot_ref[:, :1]
         onehot = jnp.where(iota((2 * NB, 4 * SLOTS_A), 1) == slot, 1.0, 0.0).astype(BF16)
         left = (dot(high, onehot).astype(BF16), dot(low, onehot).astype(BF16))
+        for load in loads[:4]:
+            load.wait()
         for c in range(lines):
             rows = arr_ref[pl.ds(c, 4 * SLOTS_A, lines), :]
             value = dot3(left, split(rows))
@@ -668,20 +699,26 @@
             stacked[0 : 2 * NB, here] = upper
             stacked[2 * NB : 4 * NB, here] = rest
             stacked[4 * NB : 6 * NB, here] = upper
-        load_panel.wait()
-        load.wait()
-
-        def patch(t, carry):
-            target = idx_ref[IN_TARGET, t]
-            line = idx_ref[IN_LINE, t]
-            panel_row = (target >> 7) * PIECE + (target & (NB - 1))
-            for half in range(2):
-                pan[half, pl.ds(panel_row, 1), :] = pan[half, pl.ds(line, 1), :]
-            source = idx_ref[IN_ROW, t] * lines
-            whole[pl.ds(target * lines, lines), :] = disp_ref[pl.ds(source, lines), :]
-            return carry
-
-        lax.fori_loop(0, idx_ref[IN_COUNT, 0], patch, 0)
+        for load in loads[4:]:
+            load.wait()
+
+    load_x(step).wait()
+    bound = (step + 1) * STEP_ROWS
+
+    def more(t):
+        return (t < idx_ref[IN_COUNT, 0]) & (idx_ref[IN_TARGET, jnp.minimum(t, 2 * NB - 1)] < bound)
+
+    def patch(t):
+        target = idx_ref[IN_TARGET, t]
+        line = idx_ref[IN_LINE, t]
+        panel_row = (target >> 7) * PIECE + (target & (NB - 1))
+        for half in range(2):
+            pan[half, pl.ds(panel_row, 1), :] = pan[half, pl.ds(line, 1), :]
+        source = idx_ref[IN_ROW, t] * lines
+        whole[pl.ds(target * lines, lines), :] = disp_ref[pl.ds(source, lines), :]
+        return t + 1
+
+    done[0] = lax.while_loop(more, patch, done[0])
 
     rows = []
     for number in range(STEP_ROWS // NB):
@@ -719,16 +756,21 @@
     return pl.pallas_call(
         update_kernel,
         grid=(16 * NB // STEP_ROWS,),
-        in_specs=[pl.BlockSpec(memory_space=pltpu.SMEM), ANY, ANY] + [vmem] * 6,
+        in_specs=[pl.BlockSpec(memory_space=pltpu.SMEM)] + [ANY] * 4 + [vmem] * 4,
         out_specs=pl.BlockSpec((STEP_ROWS * lines, NB), lambda i: (i, 0)),
         out_shape=jax.ShapeDtypeStruct((16 * NB * lines, NB), F32),
         scratch_shapes=[
             pltpu.VMEM((16 * NB * lines, NB), F32),
             pltpu.VMEM((2, 16 * PIECE, NB), F32),
+            pltpu.VMEM((2 * NB * lines, NB), F32),
+            pltpu.VMEM((4 * SLOTS_A * lines, NB), F32),
             pltpu.VMEM((6 * NB, NB * lines), BF16),
             pltpu.VMEM((2 * NB, NB * lines), F32),
-            pltpu.SemaphoreType.DMA,
-            pltpu.SemaphoreType.DMA,
+            pltpu.SMEM((1,), jnp.int32),
+            pltpu.SemaphoreType.DMA((16 * NB // STEP_ROWS,)),
+            pltpu.SemaphoreType.DMA((2,)),
+            pltpu.SemaphoreType.DMA((2,)),
+            pltpu.SemaphoreType.DMA((4,)),
         ],
         compiler_params=pltpu.CompilerParams(vmem_limit_bytes=48 * 2**20),
         name="update",

time: 81.7 us -> 73.9 us (0.905)
  Pallas kernels: 79.6 us -> 72.1 us
    pallas_call x1, Pallas kernels: 60.3 us -> 53.2 us  [front_call(): pl.pallas_call(front_kernel, in_specs=[pl.BlockSpec(memory_space=pltpu.SM...]
where the time goes in v2:
time: 73.9 us; the launch traced here: 73.7 us
  Pallas kernels  72.1 us (98%)
  between operations  0.86 us (1%)
    pallas_call x1, Pallas kernels, front_call(): pl.pallas_call(front_kernel, in_specs=[pl.BlockSpec(memory_space=pltpu.SM...  53.2 us
    pallas_call x1, Pallas kernels, update_call(): pl.pallas_call(update_kernel, grid=(16 * NB // STEP_ROWS,), in_specs=[pl....  17 us
    pallas_call x1, Pallas kernels, index_call(): pl.pallas_call(index_kernel, out_shape=[jax.ShapeDtypeStruct((16, 2 * NB)...  1.98 us

profile of v2, /device:TPU:1, one launch (start us, length us, event | category | flops | bytes accessed | tf_op | source)
XLA Modules:
  0.0 73.7 jit_solution(2306886586549742849)
XLA Ops:
  0.0 2.0 %indices.1 = (s32[16,256]{1,0:T(8,128)S(1)}, s32[256,128]{1,0:T(8,128)S(1)}) custom-call(s32[2,128]{1,0:T(2,128)} %piv_ref.1), custom_call_target="tpu_custom_call" | custom-call | tf_op jit(solution)/shard_map/indices/pallas_call | solution.py:290
  2.0 0.5 slice.63
  3.2 53.4 %conditional.1 = (f32[4224,128]{1,0:T(8,128)}, f32[3072,128]{1,0:T(8,128)}, f32[256,256]{1,0:T(8,128)S(1)}, f32[256,256]{1,0:T(8,128)S(1)}, f32[256,256]{1,0:T(8...) conditional(s32[]{:T(128)} %bitcast.14, (s32[16,256]{1,0:T(8,128)S(1)}, ...), branch_computations={%region_0.1_spmd, %region_1.0_spmd} | conditional | flops 11506436 | bytes 244667360 | solution.py:815
  3.4 53.2 %front.1 = (f32[4224,128]{1,0:T(8,128)}, f32[3072,128]{1,0:T(8,128)}, f32[2,4,4,144,128]{4,3,2,1,0:T(8,128)S(1)}, f32[256,256]{1,0:T(8,128)S(1)}, f32[256,256]{1,0:T(8,128)S(1)}, /*index=5*/f32[256,256]{1,0:T(8,128)S(1)}) custom-call(s32[16,256]{1,0:T(8,128)S(1)} %get-tuple-element.106.idx_ref, s32[256,128]{1,0:T(8,128)S(1)} %get-tuple-element.107.slot_ref, ...), custom_call_target="tpu_custom_call" | custom-call | tf_op jit(solution)/shard_map/cond/branch_1_fun/front/pallas_call | solution.py:641
  56.6 17.0 %update.1 = f32[24576,128]{1,0:T(8,128)} custom-call(s32[16,256]{1,0:T(8,128)S(1)} %get-tuple-element.72.idx_ref, f32[24576,128]{1,0:T(8,128)} %bitcast.28, f32[2,2304,128]{2,1,0:T(8,128)S(1)} %get-tuple-element.73.panel_ref, f32[3072,128]{1,0:T(8,128)} %get-tuple-element.74.disp_in, f32[4224,128]{1,0:T(8,128)} %get-tuple-element.75.arr_in, ...), custom_call_target="tpu_custom_call" | custom-call | tf_op jit(solution)/shard_map/update/pallas_call | solution.py:756

commit v3 on v2

--- a/solution.py
+++ b/solution.py
@@ -565,7 +565,7 @@
             copy.wait_recv()
         pair.start()
 
-    events = [{2: pass_piece, 3: pass_rows, 6: pass_pieces}, {6: pass_panel}]
+    events = [{3: pass_piece, 5: pass_rows}, {0: pass_pieces, 7: pass_panel}]
     for half_number in range(2):
         def factor_step(index, carry, half_number=half_number):
             for when, event in events[half_number].items():
@@ -651,7 +651,8 @@
     )(idx, slot, x)
 
 
-STEP_ROWS = 256
+STEP_ROWS = 512
+AHEAD = 2
 
 
 def update_kernel(
@@ -681,8 +682,6 @@
             loads.append(pltpu.make_async_copy(disp_in.at[here], disp_ref.at[here], disp_sem.at[half]))
         for load in loads:
             load.start()
-        for number in range(16 * NB // STEP_ROWS):
-            load_x(number).start()
         done[0] = 0
         high, low = split(linv_ref[...])
         slot = slot_ref[:, :1]
@@ -690,6 +689,8 @@
         left = (dot(high, onehot).astype(BF16), dot(low, onehot).astype(BF16))
         for load in loads[:4]:
             load.wait()
+        for number in range(AHEAD):
+            load_x(number).start()
         for c in range(lines):
             rows = arr_ref[pl.ds(c, 4 * SLOTS_A, lines), :]
             value = dot3(left, split(rows))
@@ -701,6 +702,10 @@
             stacked[4 * NB : 6 * NB, here] = upper
         for load in loads[4:]:
             load.wait()
+
+    @pl.when(step + AHEAD < 16 * NB // STEP_ROWS)
+    def _():
+        load_x(step + AHEAD).start()
 
     load_x(step).wait()
     bound = (step + 1) * STEP_ROWS

time: 73.9 us -> 70.9 us (0.959)
  Pallas kernels: 72.1 us -> 69.2 us
    pallas_call x1, Pallas kernels: 17 us -> 14.4 us  [update_call(): pl.pallas_call(update_kernel, grid=(16 * NB // STEP_ROWS,), in_specs=[pl....]
where the time goes in v3:
time: 70.9 us; the launch traced here: 70.8 us
  Pallas kernels  69.2 us (98%)
  between operations  0.86 us (1%)
    pallas_call x1, Pallas kernels, front_call(): pl.pallas_call(front_kernel, in_specs=[pl.BlockSpec(memory_space=pltpu.SM...  52.8 us
    pallas_call x1, Pallas kernels, update_call(): pl.pallas_call(update_kernel, grid=(16 * NB // STEP_ROWS,), in_specs=[pl....  14.4 us
    pallas_call x1, Pallas kernels, index_call(): pl.pallas_call(index_kernel, out_shape=[jax.ShapeDtypeStruct((16, 2 * NB)...  1.98 us

profile of v3, /device:TPU:1, one launch (start us, length us, event | category | flops | bytes accessed | tf_op | source)
XLA Modules:
  0.0 70.8 jit_solution(13502867708114135419)
XLA Ops:
  0.0 2.0 %indices.1 = (s32[16,256]{1,0:T(8,128)S(1)}, s32[256,128]{1,0:T(8,128)S(1)}) custom-call(s32[2,128]{1,0:T(2,128)} %piv_ref.1), custom_call_target="tpu_custom_call" | custom-call | tf_op jit(solution)/shard_map/indices/pallas_call | solution.py:290
  2.0 0.5 slice.63
  3.2 53.0 %conditional.1 = (f32[4224,128]{1,0:T(8,128)}, f32[3072,128]{1,0:T(8,128)}, f32[256,256]{1,0:T(8,128)S(1)}, f32[256,256]{1,0:T(8,128)S(1)}, f32[256,256]{1,0:T(8...) conditional(s32[]{:T(128)} %bitcast.14, (s32[16,256]{1,0:T(8,128)S(1)}, ...), branch_computations={%region_0.1_spmd, %region_1.0_spmd} | conditional | flops 11506436 | bytes 244667360 | solution.py:820
  3.4 52.8 %front.1 = (f32[4224,128]{1,0:T(8,128)}, f32[3072,128]{1,0:T(8,128)}, f32[2,4,4,144,128]{4,3,2,1,0:T(8,128)S(1)}, f32[256,256]{1,0:T(8,128)S(1)}, f32[256,256]{1,0:T(8,128)S(1)}, /*index=5*/f32[256,256]{1,0:T(8,128)S(1)}) custom-call(s32[16,256]{1,0:T(8,128)S(1)} %get-tuple-element.106.idx_ref, s32[256,128]{1,0:T(8,128)S(1)} %get-tuple-element.107.slot_ref, ...), custom_call_target="tpu_custom_call" | custom-call | tf_op jit(solution)/shard_map/cond/branch_1_fun/front/pallas_call | solution.py:641
  56.2 14.4 %update.1 = f32[24576,128]{1,0:T(8,128)} custom-call(s32[16,256]{1,0:T(8,128)S(1)} %get-tuple-element.72.idx_ref, f32[24576,128]{1,0:T(8,128)} %bitcast.28, f32[2,2304,128]{2,1,0:T(8,128)S(1)} %get-tuple-element.73.panel_ref, f32[3072,128]{1,0:T(8,128)} %get-tuple-element.74.disp_in, f32[4224,128]{1,0:T(8,128)} %get-tuple-element.75.arr_in, ...), custom_call_target="tpu_custom_call" | custom-call | tf_op jit(solution)/shard_map/update/pallas_call | solution.py:761

commit v4 on v3

--- a/solution.py
+++ b/solution.py
@@ -682,6 +682,7 @@
             loads.append(pltpu.make_async_copy(disp_in.at[here], disp_ref.at[here], disp_sem.at[half]))
         for load in loads:
             load.start()
+        load_x(0).start()
         done[0] = 0
         high, low = split(linv_ref[...])
         slot = slot_ref[:, :1]
@@ -689,7 +690,7 @@
         left = (dot(high, onehot).astype(BF16), dot(low, onehot).astype(BF16))
         for load in loads[:4]:
             load.wait()
-        for number in range(AHEAD):
+        for number in range(1, AHEAD):
             load_x(number).start()
         for c in range(lines):
             rows = arr_ref[pl.ds(c, 4 * SLOTS_A, lines), :]

time: 70.9 us -> 70.8 us (level)
  no operation moved by 1% of the time
where the time goes in v4:
time: 70.8 us; the launch traced here: 70.6 us
  Pallas kernels  69 us (97%)
  between operations  0.86 us (1%)
    pallas_call x1, Pallas kernels, front_call(): pl.pallas_call(front_kernel, in_specs=[pl.BlockSpec(memory_space=pltpu.SM...  52.8 us
    pallas_call x1, Pallas kernels, update_call(): pl.pallas_call(update_kernel, grid=(16 * NB // STEP_ROWS,), in_specs=[pl....  14.2 us
    pallas_call x1, Pallas kernels, index_call(): pl.pallas_call(index_kernel, out_shape=[jax.ShapeDtypeStruct((16, 2 * NB)...  1.98 us

profile of v4, /device:TPU:1, one launch (start us, length us, event | category | flops | bytes accessed | tf_op | source)
XLA Modules:
  0.0 70.6 jit_solution(8320163574011327266)
XLA Ops:
  0.0 2.0 %indices.1 = (s32[16,256]{1,0:T(8,128)S(1)}, s32[256,128]{1,0:T(8,128)S(1)}) custom-call(s32[2,128]{1,0:T(2,128)} %piv_ref.1), custom_call_target="tpu_custom_call" | custom-call | tf_op jit(solution)/shard_map/indices/pallas_call | solution.py:290
  2.0 0.5 slice.63
  3.2 53.0 %conditional.1 = (f32[4224,128]{1,0:T(8,128)}, f32[3072,128]{1,0:T(8,128)}, f32[256,256]{1,0:T(8,128)S(1)}, f32[256,256]{1,0:T(8,128)S(1)}, f32[256,256]{1,0:T(8...) conditional(s32[]{:T(128)} %bitcast.14, (s32[16,256]{1,0:T(8,128)S(1)}, ...), branch_computations={%region_0.1_spmd, %region_1.0_spmd} | conditional | flops 11506436 | bytes 244667360 | solution.py:821
  3.4 52.8 %front.1 = (f32[4224,128]{1,0:T(8,128)}, f32[3072,128]{1,0:T(8,128)}, f32[2,4,4,144,128]{4,3,2,1,0:T(8,128)S(1)}, f32[256,256]{1,0:T(8,128)S(1)}, f32[256,256]{1,0:T(8,128)S(1)}, /*index=5*/f32[256,256]{1,0:T(8,128)S(1)}) custom-call(s32[16,256]{1,0:T(8,128)S(1)} %get-tuple-element.106.idx_ref, s32[256,128]{1,0:T(8,128)S(1)} %get-tuple-element.107.slot_ref, ...), custom_call_target="tpu_custom_call" | custom-call | tf_op jit(solution)/shard_map/cond/branch_1_fun/front/pallas_call | solution.py:641
  56.2 14.2 %update.1 = f32[24576,128]{1,0:T(8,128)} custom-call(s32[16,256]{1,0:T(8,128)S(1)} %get-tuple-element.72.idx_ref, f32[24576,128]{1,0:T(8,128)} %bitcast.28, f32[2,2304,128]{2,1,0:T(8,128)S(1)} %get-tuple-element.73.panel_ref, f32[3072,128]{1,0:T(8,128)} %get-tuple-element.74.disp_in, f32[4224,128]{1,0:T(8,128)} %get-tuple-element.75.arr_in, ...), custom_call_target="tpu_custom_call" | custom-call | tf_op jit(solution)/shard_map/update/pallas_call | solution.py:762
